TPU v7x, 512 devices: a whole 4x8x8 slice. The times are simulated.
512 devices in a mesh: section: 8 (over z_lo, x), seq: 64 (over y, z_hi, core).
Axes of the slice: x: 4, y: 8, z: 8 (z_hi: 4, z_lo: 2; z = z_hi * 2 + z_lo), core: 2. Of those that a mesh axis runs over, the one named last changes fastest.
Arguments:
- fresh_qkv: bfloat16 [8, 1024, 3, 3072], P('section', 'seq'), may hold values from -6 to 6
- stale_cache: bfloat16 [8, 64, 4, 128, 768], P('section', 'seq'), may hold values from -2.5 to 2.5
- norm_gains: float32 [8, 2, 128], P('section'), may hold values from 1 to 2.5
- hidden: bfloat16 [8, 1024, 3072], P('section', 'seq'), may hold values from -6 to 6
- gate_table: bfloat16 [8, 50, 3072], P('section'), may hold values from -4 to 4
- patch_index: int32 [8], P('section'), may hold values from 0 to 3
- step_index: int32 [8], P('section'), may hold values from 0 to 49
Outputs:
- passed: bfloat16 [8, 1024, 3072], P('section', 'seq')
All inputs are finite; a program needn't handle non-finite values.
Results may differ from a plain program's by a relative error of at most 0.0095.
Values may be sent and summed in bfloat16 or wider, within the bound.
A program may use at most 64 MiB of HBM per device.

v0:
```python
import jax
import jax.numpy as jnp
from jax import lax
from jax.sharding import PartitionSpec as P

HEADS = 24
HEAD_DIM = 128
HEAD_GROUPS = 8


def passed_along(shard, axis, by):
    count = lax.axis_size(axis)
    return lax.ppermute(shard, axis, [(i, (i + by) % count) for i in range(count)])


def normed(values, norm_gain):
    values = values.astype(jnp.float32)
    factor = lax.rsqrt(jnp.mean(values * values, axis=-1, keepdims=True) + 1e-06)
    return (values * factor * norm_gain).astype(jnp.bfloat16)


def attend(queries, local_keys):
    stale_keys, stale_values, keep_mask, fresh_keys, fresh_values = local_keys
    row_count = queries.shape[0]
    head_count = stale_keys.shape[1]
    head_size = stale_keys.shape[2]
    shaped = queries.reshape(row_count, head_count, head_size)
    factor = head_size ** (-0.5)
    stale_scores = (
        jnp.einsum("rhd,khd->hrk", shaped, stale_keys, preferred_element_type=jnp.float32) * factor
    )
    stale_weights = jnp.exp(stale_scores) * keep_mask
    fresh_scores = (
        jnp.einsum("rhd,khd->hrk", shaped, fresh_keys, preferred_element_type=jnp.float32) * factor
    )
    fresh_weights = jnp.exp(fresh_scores)
    totals = jnp.sum(stale_weights, axis=-1) + jnp.sum(fresh_weights, axis=-1)
    summed = jnp.einsum(
        "hrk,khd->rhd",
        stale_weights.astype(jnp.bfloat16),
        stale_values,
        preferred_element_type=jnp.float32,
    )
    summed = summed + jnp.einsum(
        "hrk,khd->rhd",
        fresh_weights.astype(jnp.bfloat16),
        fresh_values,
        preferred_element_type=jnp.float32,
    )
    return (summed.reshape(row_count, head_count * head_size), totals.T)


def shards(fresh_qkv, stale_cache, norm_gains, hidden, gate_table, patch_index, step_index):
    seq_count = lax.axis_size("seq")
    groups = seq_count // HEAD_GROUPS
    tok_rows = hidden.shape[1]
    sub_rows = tok_rows // groups
    full_width = hidden.shape[2]
    group_width = full_width // HEAD_GROUPS
    group_heads = group_width // HEAD_DIM
    all_rows = seq_count * sub_rows
    patches = stale_cache.shape[2]
    triple = fresh_qkv[0].reshape(tok_rows, 3, HEADS, HEAD_DIM)
    queries = normed(triple[:, 0], norm_gains[0, 0])
    key_normed = normed(triple[:, 1], norm_gains[0, 1])
    stacked = jnp.stack([queries, key_normed, triple[:, 2]], axis=1)
    stacked = stacked.reshape(groups, sub_rows, 3, HEAD_GROUPS, group_width)
    outgoing = stacked.transpose(0, 3, 1, 2, 4).reshape(seq_count, sub_rows, 3 * group_width)
    arrived = lax.all_to_all(outgoing, "seq", split_axis=0, concat_axis=0, tiled=True)
    arrived = arrived.reshape(all_rows, 3, group_width)
    own_queries = arrived[:, 0]
    fresh_keys = arrived[:, 1].reshape(all_rows, group_heads, HEAD_DIM)
    fresh_values = arrived[:, 2].reshape(all_rows, group_heads, HEAD_DIM)
    own_cache = stale_cache[0, 0]
    stale_keys = own_cache[:, :, :group_width].reshape(patches * all_rows, group_heads, HEAD_DIM)
    stale_values = own_cache[:, :, group_width:].reshape(patches * all_rows, group_heads, HEAD_DIM)
    keep_mask = jnp.repeat((jnp.arange(patches) != patch_index[0]).astype(jnp.float32), all_rows)
    keep_mask = keep_mask.reshape(1, 1, patches * all_rows)
    local_keys = (stale_keys, stale_values, keep_mask, fresh_keys, fresh_values)
    first_num, first_den = attend(own_queries, local_keys)
    position = lax.axis_index("seq") // HEAD_GROUPS
    store_num = jnp.zeros((groups, all_rows, group_width), jnp.float32)
    store_den = jnp.zeros((groups, all_rows, group_heads), jnp.float32)
    store_num = lax.dynamic_update_slice(store_num, first_num[None], (position, 0, 0))
    store_den = lax.dynamic_update_slice(store_den, first_den[None], (position, 0, 0))

    def visiting(turn_index, loop_state):
        moving, slot_num, slot_den = loop_state
        moving = passed_along(moving, "seq", HEAD_GROUPS)
        anchor = (position - turn_index) % groups
        part_num, part_den = attend(moving, local_keys)
        slot_num = lax.dynamic_update_slice(slot_num, part_num[None], (anchor, 0, 0))
        slot_den = lax.dynamic_update_slice(slot_den, part_den[None], (anchor, 0, 0))
        return (moving, slot_num, slot_den)

    moving, store_num, store_den = lax.fori_loop(
        1, groups, visiting, (own_queries, store_num, store_den)
    )
    out_num = store_num.reshape(groups, seq_count, sub_rows, group_width).transpose(1, 0, 2, 3)
    out_den = store_den.reshape(groups, seq_count, sub_rows, group_heads).transpose(1, 0, 2, 3)
    back_num, back_den = (
        lax.all_to_all(
            out_num.astype(jnp.bfloat16), "seq", split_axis=0, concat_axis=0, tiled=True
        ).astype(out_num.dtype),
        lax.all_to_all(
            out_den.astype(jnp.bfloat16), "seq", split_axis=0, concat_axis=0, tiled=True
        ).astype(out_den.dtype),
    )
    back_num = back_num.reshape(groups, HEAD_GROUPS, groups, sub_rows, group_width).sum(axis=0)
    back_den = back_den.reshape(groups, HEAD_GROUPS, groups, sub_rows, group_heads).sum(axis=0)
    result = (
        back_num.reshape(HEAD_GROUPS, groups, sub_rows, group_heads, HEAD_DIM) / back_den[..., None]
    )
    attention = result.astype(jnp.bfloat16).transpose(1, 2, 0, 3, 4).reshape(tok_rows, full_width)
    selector = (jnp.arange(gate_table.shape[1]) == step_index[0]).astype(jnp.bfloat16)
    gate_row = jnp.dot(selector, gate_table[0], preferred_element_type=jnp.float32)
    mixed = (hidden[0].astype(jnp.float32) + gate_row * attention.astype(jnp.float32)).astype(
        jnp.bfloat16
    )
    passed = passed_along(mixed, "section", 1)
    return passed[None]


def solution(mesh):
    return jax.shard_map(
        shards,
        mesh=mesh,
        in_specs=(
            P("section", "seq", None, None),
            P("section", "seq", None, None, None),
            P("section", None, None),
            P("section", "seq", None),
            P("section", None, None),
            P("section"),
            P("section"),
        ),
        out_specs=P("section", "seq", None),
        check_vma=False,
    )
```

profile of v0, /device:TPU:1, one launch (start us, length us, event | category | flops | bytes accessed | tf_op | source)
XLA Modules:
  0.0 158.4 jit_solution(10491214660056793813)
XLA Ops:
  0.0 1.1 copy.90
  1.7 0.3 copy.85
  2.0 1.0 reshape.102
  3.0 17.6 %all-to-all-start = ((bf16[64,2,1152]{2,1,0:T(2,128)(2,1)}), bf16[64,2,1152]{2,1,0:T(2,128)(2,1)S(1)}, u32[]{:S(2)}, u32[]{:S(2)}) async-start(bf16[64,2,1152]{2,1,0:T(2,128)(2,1)} %reshape.102), calls=%async_computation | async-start | bytes 589824 | tf_op jit(solution)/shard_map/all_to_all | solution.py:69
  22.5 14.2 %all-to-all-done = bf16[64,2,1152]{2,1,0:T(2,128)(2,1)S(1)} async-done(((bf16[64,2,1152]{2,1,0:T(2,128)(2,1)}), bf16[64,2,1152]{2,1,0:T(2,128)(2,1)S(1)}, u32[]{:S(2)}, u32[]{:S(2)}) %all-to-all-start) | async-done | bytes 294944 | tf_op jit(solution)/shard_map/all_to_all | solution.py:69
  36.9 0.4 fusion.30
  37.8 0.3 fusion.32
  38.1 0.4 fusion.31
  38.9 0.3 fusion.11
  39.3 55.0 %while.20 = (s32[]{:T(128)}, bf16[128,384]{0,1:T(8,128)(2,1)S(1)}, bf16[8,128,384]{1,2,0:T(8,128)(2,1)S(1)}, bf16[8,128,3]{1,2,0:T(4,128)(2,1)S(1)}, bf16[512,3,...) while((s32[]{:T(128)}, bf16[128,384]{0,1:T(8,128)(2,1)S(1)}, ...), condition=%wide.region_7.8_spmd.clone, body=%wide.region_4.7_spmd.clone.sunk | while | flops 126860944 | bytes 3454304 | solution.py:96
  39.3 2.6 %collective-permute-start = (bf16[128,384]{0,1:T(8,128)(2,1)S(1)}, bf16[128,384]{0,1:T(8,128)(2,1)S(1)}, u32[]{:S(2)}, u32[]{:S(2)}) collective-permute-start(bf16[128,384]{0,1:T(8,128)(2,1)S(1)} %get-tuple-element.437), channel_id=1, source_target_pairs={{0,8},{1,9},{2,10},{3,11},{4,12},{5,13},{6,14},{7,15},{8,16},{9,17... | collective-permute-start | bytes 294920 | tf_op jit(solution)/shard_map/while/body/eval_jaxpr/ppermute | solution.py:13
  42.0 4.7 %collective-permute-done = bf16[128,384]{0,1:T(8,128)(2,1)S(1)} collective-permute-done((bf16[128,384]{0,1:T(8,128)(2,1)S(1)}, bf16[128,384]{0,1:T(8,128)(2,1)S(1)}, u32[]{:S(2)}, u32[]{:S(2)}) %collective-permute-start) | collective-permute-done | bytes 98336 | tf_op jit(solution)/shard_map/while/body/eval_jaxpr/ppermute | solution.py:13
  46.9 0.4 fusion.68
  47.3 0.3 fusion.69
  47.9 1.9 %collective-permute-start = (bf16[128,384]{0,1:T(8,128)(2,1)S(1)}, bf16[128,384]{0,1:T(8,128)(2,1)S(1)}, u32[]{:S(2)}, u32[]{:S(2)}) collective-permute-start(bf16[128,384]{0,1:T(8,128)(2,1)S(1)} %get-tuple-element.437), channel_id=1, source_target_pairs={{0,8},{1,9},{2,10},{3,11},{4,12},{5,13},{6,14},{7,15},{8,16},{9,17... | collective-permute-start | bytes 294920 | tf_op jit(solution)/shard_map/while/body/eval_jaxpr/ppermute | solution.py:13
  49.9 4.6 %collective-permute-done = bf16[128,384]{0,1:T(8,128)(2,1)S(1)} collective-permute-done((bf16[128,384]{0,1:T(8,128)(2,1)S(1)}, bf16[128,384]{0,1:T(8,128)(2,1)S(1)}, u32[]{:S(2)}, u32[]{:S(2)}) %collective-permute-start) | collective-permute-done | bytes 98336 | tf_op jit(solution)/shard_map/while/body/eval_jaxpr/ppermute | solution.py:13
  54.6 0.4 fusion.68
  55.1 0.3 fusion.69
  55.6 1.9 %collective-permute-start = (bf16[128,384]{0,1:T(8,128)(2,1)S(1)}, bf16[128,384]{0,1:T(8,128)(2,1)S(1)}, u32[]{:S(2)}, u32[]{:S(2)}) collective-permute-start(bf16[128,384]{0,1:T(8,128)(2,1)S(1)} %get-tuple-element.437), channel_id=1, source_target_pairs={{0,8},{1,9},{2,10},{3,11},{4,12},{5,13},{6,14},{7,15},{8,16},{9,17... | collective-permute-start | bytes 294920 | tf_op jit(solution)/shard_map/while/body/eval_jaxpr/ppermute | solution.py:13
  57.6 4.6 %collective-permute-done = bf16[128,384]{0,1:T(8,128)(2,1)S(1)} collective-permute-done((bf16[128,384]{0,1:T(8,128)(2,1)S(1)}, bf16[128,384]{0,1:T(8,128)(2,1)S(1)}, u32[]{:S(2)}, u32[]{:S(2)}) %collective-permute-start) | collective-permute-done | bytes 98336 | tf_op jit(solution)/shard_map/while/body/eval_jaxpr/ppermute | solution.py:13
  62.4 0.4 fusion.68
  62.8 0.3 fusion.69
  63.3 1.9 %collective-permute-start = (bf16[128,384]{0,1:T(8,128)(2,1)S(1)}, bf16[128,384]{0,1:T(8,128)(2,1)S(1)}, u32[]{:S(2)}, u32[]{:S(2)}) collective-permute-start(bf16[128,384]{0,1:T(8,128)(2,1)S(1)} %get-tuple-element.437), channel_id=1, source_target_pairs={{0,8},{1,9},{2,10},{3,11},{4,12},{5,13},{6,14},{7,15},{8,16},{9,17... | collective-permute-start | bytes 294920 | tf_op jit(solution)/shard_map/while/body/eval_jaxpr/ppermute | solution.py:13
  65.3 4.6 %collective-permute-done = bf16[128,384]{0,1:T(8,128)(2,1)S(1)} collective-permute-done((bf16[128,384]{0,1:T(8,128)(2,1)S(1)}, bf16[128,384]{0,1:T(8,128)(2,1)S(1)}, u32[]{:S(2)}, u32[]{:S(2)}) %collective-permute-start) | collective-permute-done | bytes 98336 | tf_op jit(solution)/shard_map/while/body/eval_jaxpr/ppermute | solution.py:13
  70.1 0.4 fusion.68
  70.5 0.3 fusion.69
  71.1 1.9 %collective-permute-start = (bf16[128,384]{0,1:T(8,128)(2,1)S(1)}, bf16[128,384]{0,1:T(8,128)(2,1)S(1)}, u32[]{:S(2)}, u32[]{:S(2)}) collective-permute-start(bf16[128,384]{0,1:T(8,128)(2,1)S(1)} %get-tuple-element.437), channel_id=1, source_target_pairs={{0,8},{1,9},{2,10},{3,11},{4,12},{5,13},{6,14},{7,15},{8,16},{9,17... | collective-permute-start | bytes 294920 | tf_op jit(solution)/shard_map/while/body/eval_jaxpr/ppermute | solution.py:13
  73.1 4.6 %collective-permute-done = bf16[128,384]{0,1:T(8,128)(2,1)S(1)} collective-permute-done((bf16[128,384]{0,1:T(8,128)(2,1)S(1)}, bf16[128,384]{0,1:T(8,128)(2,1)S(1)}, u32[]{:S(2)}, u32[]{:S(2)}) %collective-permute-start) | collective-permute-done | bytes 98336 | tf_op jit(solution)/shard_map/while/body/eval_jaxpr/ppermute | solution.py:13
  77.8 0.4 fusion.68
  78.3 0.3 fusion.69
  78.8 1.9 %collective-permute-start = (bf16[128,384]{0,1:T(8,128)(2,1)S(1)}, bf16[128,384]{0,1:T(8,128)(2,1)S(1)}, u32[]{:S(2)}, u32[]{:S(2)}) collective-permute-start(bf16[128,384]{0,1:T(8,128)(2,1)S(1)} %get-tuple-element.437), channel_id=1, source_target_pairs={{0,8},{1,9},{2,10},{3,11},{4,12},{5,13},{6,14},{7,15},{8,16},{9,17... | collective-permute-start | bytes 294920 | tf_op jit(solution)/shard_map/while/body/eval_jaxpr/ppermute | solution.py:13
  80.8 4.6 %collective-permute-done = bf16[128,384]{0,1:T(8,128)(2,1)S(1)} collective-permute-done((bf16[128,384]{0,1:T(8,128)(2,1)S(1)}, bf16[128,384]{0,1:T(8,128)(2,1)S(1)}, u32[]{:S(2)}, u32[]{:S(2)}) %collective-permute-start) | collective-permute-done | bytes 98336 | tf_op jit(solution)/shard_map/while/body/eval_jaxpr/ppermute | solution.py:13
  85.6 0.4 fusion.68
  86.0 0.3 fusion.69
  86.5 1.9 %collective-permute-start = (bf16[128,384]{0,1:T(8,128)(2,1)S(1)}, bf16[128,384]{0,1:T(8,128)(2,1)S(1)}, u32[]{:S(2)}, u32[]{:S(2)}) collective-permute-start(bf16[128,384]{0,1:T(8,128)(2,1)S(1)} %get-tuple-element.437), channel_id=1, source_target_pairs={{0,8},{1,9},{2,10},{3,11},{4,12},{5,13},{6,14},{7,15},{8,16},{9,17... | collective-permute-start | bytes 294920 | tf_op jit(solution)/shard_map/while/body/eval_jaxpr/ppermute | solution.py:13
  88.5 4.6 %collective-permute-done = bf16[128,384]{0,1:T(8,128)(2,1)S(1)} collective-permute-done((bf16[128,384]{0,1:T(8,128)(2,1)S(1)}, bf16[128,384]{0,1:T(8,128)(2,1)S(1)}, u32[]{:S(2)}, u32[]{:S(2)}) %collective-permute-start) | collective-permute-done | bytes 98336 | tf_op jit(solution)/shard_map/while/body/eval_jaxpr/ppermute | solution.py:13
  93.3 0.4 fusion.68
  93.8 0.3 fusion.69
  94.4 0.7 copy.73
  95.2 12.3 %all-to-all-start.2 = ((bf16[64,8,2,3]{1,2,3,0:T(2,128)(2,1)}), bf16[64,8,2,3]{1,2,3,0:T(2,128)(2,1)S(1)}, u32[]{:S(2)}, u32[]{:S(2)}) async-start(bf16[64,8,2,3]{1,2,3,0:T(2,128)(2,1)} %copy.73), calls=%async_computation.2 | async-start | bytes 196608 | tf_op jit(solution)/shard_map/all_to_all | solution.py:105
  107.5 1.3 copy.71
  108.8 11.6 %all-to-all-done.2 = bf16[64,8,2,3]{1,2,3,0:T(2,128)(2,1)S(1)} async-done(((bf16[64,8,2,3]{1,2,3,0:T(2,128)(2,1)}), bf16[64,8,2,3]{1,2,3,0:T(2,128)(2,1)S(1)}, u32[]{:S(2)}, u32[]{:S(2)}) %all-to-all-start.2) | async-done | bytes 6176 | tf_op jit(solution)/shard_map/all_to_all | solution.py:105
  120.5 4.5 %all-to-all-start.1 = ((bf16[64,8,2,384]{3,1,2,0:T(8,128)(2,1)}), bf16[64,8,2,384]{3,1,2,0:T(8,128)(2,1)S(1)}, u32[]{:S(2)}, u32[]{:S(2)}) async-start(bf16[64,8,2,384]{3,1,2,0:T(8,128)(2,1)} %bitcast.21), calls=%async_computation.1 | async-start | bytes 1572864 | tf_op jit(solution)/shard_map/all_to_all | solution.py:102
  126.1 23.1 %all-to-all-done.1 = bf16[64,8,2,384]{3,1,2,0:T(8,128)(2,1)S(1)} async-done(((bf16[64,8,2,384]{3,1,2,0:T(8,128)(2,1)}), bf16[64,8,2,384]{3,1,2,0:T(8,128)(2,1)S(1)}, u32[]{:S(2)}, u32[]{:S(2)}) %all-to-all-start.1) | async-done | bytes 786464 | tf_op jit(solution)/shard_map/all_to_all | solution.py:102
  149.7 0.5 copy-done.2
  150.2 3.1 %collective-permute-start.1 = (bf16[16,3072]{1,0:T(8,128)(2,1)S(1)}, bf16[16,3072]{1,0:T(8,128)(2,1)S(1)}, u32[]{:S(2)}, u32[]{:S(2)}) collective-permute-start(bf16[16,3072]{1,0:T(8,128)(2,1)S(1)} %fusion.21), channel_id=1, source_target_pairs={{0,64},{64,128},{128,192},{192,256},{256,320},{320,384},{384,448},... | collective-permute-start | bytes 294920 | tf_op jit(solution)/shard_map/ppermute | solution.py:13
  153.4 4.4 %collective-permute-done.1 = bf16[16,3072]{1,0:T(8,128)(2,1)S(1)} collective-permute-done((bf16[16,3072]{1,0:T(8,128)(2,1)S(1)}, bf16[16,3072]{1,0:T(8,128)(2,1)S(1)}, u32[]{:S(2)}, u32[]{:S(2)}) %collective-permute-start.1) | collective-permute-done | bytes 98336 | tf_op jit(solution)/shard_map/ppermute | solution.py:13
  157.7 0.6 copy.110
  (86 shorter events, 7.5 us)
Async XLA Ops:
  0.0 125.6 %copy-start = (bf16[1,50,3072]{2,1,0:T(8,128)(2,1)S(1)}, bf16[1,50,3072]{2,1,0:T(8,128)(2,1)}, u32[]{:S(2)}) copy-start(bf16[1,50,3072]{2,1,0:T(8,128)(2,1)} %param.13) | copy-start | bytes 921604
  0.0 1.3 copy-start.3
  2.0 18.6 %copy-start.1 = (bf16[1,1,4,128,768]{4,3,2,1,0:T(8,128)(2,1)S(1)}, bf16[1,1,4,128,768]{4,3,2,1,0:T(8,128)(2,1)}, u32[]{:S(2)}) copy-start(bf16[1,1,4,128,768]{4,3,2,1,0:T(8,128)(2,1)} %param.10) | copy-start | bytes 2359300
  3.0 33.8 %all-to-all-start = ((bf16[64,2,1152]{2,1,0:T(2,128)(2,1)}), bf16[64,2,1152]{2,1,0:T(2,128)(2,1)S(1)}, u32[]{:S(2)}, u32[]{:S(2)}) async-start(bf16[64,2,1152]{2,1,0:T(2,128)(2,1)} %reshape.102), calls=%async_computation | async-start | bytes 589824 | tf_op jit(solution)/shard_map/all_to_all | solution.py:69
  39.3 7.4 %collective-permute-start = (bf16[128,384]{0,1:T(8,128)(2,1)S(1)}, bf16[128,384]{0,1:T(8,128)(2,1)S(1)}, u32[]{:S(2)}, u32[]{:S(2)}) collective-permute-start(bf16[128,384]{0,1:T(8,128)(2,1)S(1)} %get-tuple-element.437), channel_id=1, source_target_pairs={{0,8},{1,9},{2,10},{3,11},{4,12},{5,13},{6,14},{7,15},{8,16},{9,17... | collective-permute-start | bytes 294920 | tf_op jit(solution)/shard_map/while/body/eval_jaxpr/ppermute | solution.py:13
  47.9 6.6 %collective-permute-start = (bf16[128,384]{0,1:T(8,128)(2,1)S(1)}, bf16[128,384]{0,1:T(8,128)(2,1)S(1)}, u32[]{:S(2)}, u32[]{:S(2)}) collective-permute-start(bf16[128,384]{0,1:T(8,128)(2,1)S(1)} %get-tuple-element.437), channel_id=1, source_target_pairs={{0,8},{1,9},{2,10},{3,11},{4,12},{5,13},{6,14},{7,15},{8,16},{9,17... | collective-permute-start | bytes 294920 | tf_op jit(solution)/shard_map/while/body/eval_jaxpr/ppermute | solution.py:13
  55.6 6.6 %collective-permute-start = (bf16[128,384]{0,1:T(8,128)(2,1)S(1)}, bf16[128,384]{0,1:T(8,128)(2,1)S(1)}, u32[]{:S(2)}, u32[]{:S(2)}) collective-permute-start(bf16[128,384]{0,1:T(8,128)(2,1)S(1)} %get-tuple-element.437), channel_id=1, source_target_pairs={{0,8},{1,9},{2,10},{3,11},{4,12},{5,13},{6,14},{7,15},{8,16},{9,17... | collective-permute-start | bytes 294920 | tf_op jit(solution)/shard_map/while/body/eval_jaxpr/ppermute | solution.py:13
  63.3 6.6 %collective-permute-start = (bf16[128,384]{0,1:T(8,128)(2,1)S(1)}, bf16[128,384]{0,1:T(8,128)(2,1)S(1)}, u32[]{:S(2)}, u32[]{:S(2)}) collective-permute-start(bf16[128,384]{0,1:T(8,128)(2,1)S(1)} %get-tuple-element.437), channel_id=1, source_target_pairs={{0,8},{1,9},{2,10},{3,11},{4,12},{5,13},{6,14},{7,15},{8,16},{9,17... | collective-permute-start | bytes 294920 | tf_op jit(solution)/shard_map/while/body/eval_jaxpr/ppermute | solution.py:13
  71.1 6.6 %collective-permute-start = (bf16[128,384]{0,1:T(8,128)(2,1)S(1)}, bf16[128,384]{0,1:T(8,128)(2,1)S(1)}, u32[]{:S(2)}, u32[]{:S(2)}) collective-permute-start(bf16[128,384]{0,1:T(8,128)(2,1)S(1)} %get-tuple-element.437), channel_id=1, source_target_pairs={{0,8},{1,9},{2,10},{3,11},{4,12},{5,13},{6,14},{7,15},{8,16},{9,17... | collective-permute-start | bytes 294920 | tf_op jit(solution)/shard_map/while/body/eval_jaxpr/ppermute | solution.py:13
  78.8 6.6 %collective-permute-start = (bf16[128,384]{0,1:T(8,128)(2,1)S(1)}, bf16[128,384]{0,1:T(8,128)(2,1)S(1)}, u32[]{:S(2)}, u32[]{:S(2)}) collective-permute-start(bf16[128,384]{0,1:T(8,128)(2,1)S(1)} %get-tuple-element.437), channel_id=1, source_target_pairs={{0,8},{1,9},{2,10},{3,11},{4,12},{5,13},{6,14},{7,15},{8,16},{9,17... | collective-permute-start | bytes 294920 | tf_op jit(solution)/shard_map/while/body/eval_jaxpr/ppermute | solution.py:13
  86.5 6.6 %collective-permute-start = (bf16[128,384]{0,1:T(8,128)(2,1)S(1)}, bf16[128,384]{0,1:T(8,128)(2,1)S(1)}, u32[]{:S(2)}, u32[]{:S(2)}) collective-permute-start(bf16[128,384]{0,1:T(8,128)(2,1)S(1)} %get-tuple-element.437), channel_id=1, source_target_pairs={{0,8},{1,9},{2,10},{3,11},{4,12},{5,13},{6,14},{7,15},{8,16},{9,17... | collective-permute-start | bytes 294920 | tf_op jit(solution)/shard_map/while/body/eval_jaxpr/ppermute | solution.py:13
  95.2 25.3 %all-to-all-start.2 = ((bf16[64,8,2,3]{1,2,3,0:T(2,128)(2,1)}), bf16[64,8,2,3]{1,2,3,0:T(2,128)(2,1)S(1)}, u32[]{:S(2)}, u32[]{:S(2)}) async-start(bf16[64,8,2,3]{1,2,3,0:T(2,128)(2,1)} %copy.73), calls=%async_computation.2 | async-start | bytes 196608 | tf_op jit(solution)/shard_map/all_to_all | solution.py:105
  120.5 28.7 %all-to-all-start.1 = ((bf16[64,8,2,384]{3,1,2,0:T(8,128)(2,1)}), bf16[64,8,2,384]{3,1,2,0:T(8,128)(2,1)S(1)}, u32[]{:S(2)}, u32[]{:S(2)}) async-start(bf16[64,8,2,384]{3,1,2,0:T(8,128)(2,1)} %bitcast.21), calls=%async_computation.1 | async-start | bytes 1572864 | tf_op jit(solution)/shard_map/all_to_all | solution.py:102
  149.3 0.9 copy-start.2
  150.2 7.5 %collective-permute-start.1 = (bf16[16,3072]{1,0:T(8,128)(2,1)S(1)}, bf16[16,3072]{1,0:T(8,128)(2,1)S(1)}, u32[]{:S(2)}, u32[]{:S(2)}) collective-permute-start(bf16[16,3072]{1,0:T(8,128)(2,1)S(1)} %fusion.21), channel_id=1, source_target_pairs={{0,64},{64,128},{128,192},{192,256},{256,320},{320,384},{384,448},... | collective-permute-start | bytes 294920 | tf_op jit(solution)/shard_map/ppermute | solution.py:13
where the time goes:
time: 161 us; the launch traced here: 158 us
  waiting for transfers between devices  85.4 us (53%)
  starting transfers between devices  51.7 us (32%)
  local copies, waits for them, and re-layouts  9.5 us (6%)
  matrix products  8.8 us (5%)
  between operations  1.64 us (1%)
    ppermute x8, waiting for transfers between devices, passed_along(): lax.ppermute(shard, axis, [(i, (i + by) % count) for i in range(count)])  36.5 us
    all_to_all x1, waiting for transfers between devices, shards(): lax.all_to_all(out_num.astype(jnp.bfloat16), 'seq', split_axis=0, concat_...  23.1 us
    all_to_all x1, starting transfers between devices, shards(): lax.all_to_all(outgoing, 'seq', split_axis=0, concat_axis=0, tiled=True)  17.6 us
    ppermute x8, starting transfers between devices, passed_along(): lax.ppermute(shard, axis, [(i, (i + by) % count) for i in range(count)])  17.3 us
    all_to_all x1, waiting for transfers between devices, shards(): lax.all_to_all(outgoing, 'seq', split_axis=0, concat_axis=0, tiled=True)  14.2 us
    all_to_all x1, starting transfers between devices, shards(): lax.all_to_all(out_den.astype(jnp.bfloat16), 'seq', split_axis=0, concat_...  12.3 us
    all_to_all x1, waiting for transfers between devices, shards(): lax.all_to_all(out_den.astype(jnp.bfloat16), 'seq', split_axis=0, concat_...  11.6 us
    all_to_all x1, starting transfers between devices, shards(): lax.all_to_all(out_num.astype(jnp.bfloat16), 'seq', split_axis=0, concat_...  4.47 us
  transfers between devices with their start and end apart: 11, of which 11 were waited for; matrix products, arithmetic and copies ran while one was open for 2% of the time, Pallas kernels for 0%

commit v1 on v0

v1 whole, which is shorter than its diff:
```python
import functools

import jax
import jax.numpy as jnp
from jax import lax
from jax.experimental import pallas as pl
from jax.experimental.pallas import tpu as pltpu
from jax.sharding import PartitionSpec as P

HEADS = 24
HEAD_DIM = 128
HEAD_GROUPS = 8
MESH = pl.DeviceIdType.MESH
F32 = jnp.float32
BF16 = jnp.bfloat16


def kernel(
    sections,
    seq_count,
    fresh,
    stale,
    gains,
    hidden,
    gate,
    patch,
    step,
    out,
    raw,
    old,
    gate_all,
    gate_row,
    q_out,
    k_out,
    q_all,
    keys,
    values_t,
    v_in,
    h_in,
    part,
    back,
    send,
    mixed,
    local_sem,
    own_sem,
    first_send,
    first_recv,
    turn_send,
    turn_recv,
    back_send,
    back_recv,
    out_send,
    out_recv,
):
    groups = HEAD_GROUPS
    ring = seq_count // groups
    reach = ring // 2
    heads = q_out.shape[1]
    toks = q_out.shape[2]
    dim = HEAD_DIM
    width = heads * dim
    block = groups * toks
    stale_rows = old.shape[1]
    kept = old.shape[0] - 1
    stale_keys = kept * stale_rows

    sec = lax.axis_index("section")
    me = lax.axis_index("seq")
    y = me // groups
    a = me % groups
    up = lax.rem(y + 1, ring) * groups + a
    down = lax.rem(y + ring - 1, ring) * groups + a
    next_sec = lax.rem(sec + 1, sections)
    prev_sec = lax.rem(sec + sections - 1, sections)

    def peer(d):
        return y * groups + lax.rem(a + d, groups)

    def ring_step(d):
        return lax.rem(y + ring + 1 - 2 * d, ring) * groups + a

    raw_copy = pltpu.make_async_copy(fresh.at[0, pl.ds(0, 2)], raw, local_sem.at[0])
    raw_copy.start()

    barrier = pltpu.get_barrier_semaphore()
    for d in range(1, groups):
        pl.semaphore_signal(barrier, inc=1, device_id=(sec, peer(d)), device_id_type=MESH)
    for other in (up, down):
        pl.semaphore_signal(barrier, inc=1, device_id=(sec, other), device_id_type=MESH)
    for d in range(groups):
        pl.semaphore_signal(barrier, inc=1, device_id=(prev_sec, peer(d)), device_id_type=MESH)

    old_copy = pltpu.make_async_copy(stale.at[0, 0], old, local_sem.at[1])
    old_copy.start()
    gate_copy = pltpu.make_async_copy(gate.at[0], gate_all, local_sem.at[2])
    gate_copy.start()
    mine = pl.ds(pl.multiple_of(a * toks, toks), toks)
    my_keys = pl.ds(pl.multiple_of(stale_keys + a * toks, toks), toks)
    my_cols = pl.ds(pl.multiple_of(a * width, dim), width)
    own_v = pltpu.make_async_copy(fresh.at[0, 2, :, my_cols], v_in.at[mine], own_sem.at[0])
    own_v.start()
    own_h = pltpu.make_async_copy(hidden.at[0, :, my_cols], h_in.at[mine], own_sem.at[1])
    own_h.start()

    raw_copy.wait()

    def norm(which, stage):
        gain = gains[0, which : which + 1, :]
        for g in range(groups):
            for i in range(heads):
                col = (g * heads + i) * dim
                x = raw[which, :, col : col + dim].astype(F32)
                factor = lax.rsqrt(jnp.mean(x * x, axis=-1, keepdims=True) + 1e-06)
                stage[g, i] = (x * factor * gain).astype(BF16)

    norm(0, q_out)

    pl.semaphore_wait(barrier, 2 * groups + 1)

    def first_copy(kind, d):
        to = lax.rem(a + d, groups)
        cols = pl.ds(pl.multiple_of(to * width, dim), width)
        src, dst = (
            (lambda: q_out.at[to], lambda: q_all.at[0, :, 0, mine, :]),
            (lambda: k_out.at[to], lambda: keys.at[:, my_keys, :]),
            (lambda: fresh.at[0, 2, :, cols], lambda: v_in.at[mine]),
            (lambda: hidden.at[0, :, cols], lambda: h_in.at[mine]),
        )[kind]
        return pltpu.make_async_remote_copy(
            src_ref=src(),
            dst_ref=dst(),
            send_sem=first_send.at[kind, d],
            recv_sem=first_recv.at[kind, d],
            device_id=(sec, peer(d)),
            device_id_type=MESH,
        )

    def first_arrived(kind, d):
        source = lax.rem(a + groups - d, groups)
        rows = pl.ds(pl.multiple_of(source * toks, toks), toks)
        key_rows = pl.ds(pl.multiple_of(stale_keys + source * toks, toks), toks)
        dst = (
            lambda: q_all.at[0, :, 0, rows, :],
            lambda: keys.at[:, key_rows, :],
            lambda: v_in.at[rows],
            lambda: h_in.at[rows],
        )[kind]()
        pltpu.make_async_remote_copy(
            src_ref=dst,
            dst_ref=dst,
            send_sem=first_send.at[kind, d],
            recv_sem=first_recv.at[kind, d],
            device_id=(sec, peer(d)),
            device_id_type=MESH,
        ).wait_recv()

    for d in range(1, groups):
        first_copy(0, d).start()
    q_all[0, :, 0, mine, :] = q_out[a]
    norm(1, k_out)
    for d in range(1, groups):
        first_copy(1, d).start()
    keys[:, my_keys, :] = k_out[a]
    for kind in (2, 3):
        for d in range(1, groups):
            first_copy(kind, d).start()

    def turn(r, i, d):
        far = r + 1 == reach
        return pltpu.make_async_remote_copy(
            src_ref=q_all.at[r, i, 0 if r == 0 else d],
            dst_ref=q_all.at[0, i, 1] if far else q_all.at[r + 1, i, d],
            send_sem=turn_send.at[r, i, d],
            recv_sem=turn_recv.at[r + 1, i, 0 if far else d],
            device_id=(sec, ring_step(d)),
            device_id_type=MESH,
        )

    def turn_arrived(r, i, d):
        far = r == reach
        dst = q_all.at[0, i, 1] if far else q_all.at[r, i, d]
        pltpu.make_async_remote_copy(
            src_ref=dst,
            dst_ref=dst,
            send_sem=turn_send.at[0, i, 0],
            recv_sem=turn_recv.at[r, i, 0 if far else d],
            device_id=(sec, up),
            device_id_type=MESH,
        ).wait_recv()

    def far_way(i):
        return i % 2

    for d in range(1, groups):
        first_arrived(0, d)
    for i in range(heads):
        for d in range(2):
            turn(0, i, d).start()

    old_copy.wait()
    skip = patch[0]

    for n in range(kept):
        m = n + (n >= skip).astype(jnp.int32)
        rows = slice(n * stale_rows, (n + 1) * stale_rows)
        for i in range(heads):
            keys[i, rows, :] = old[m, :, i * dim : (i + 1) * dim]
            values_t[i, 0:dim, rows] = old[m, :, width + i * dim : width + (i + 1) * dim].T
    for i in range(heads):
        values_t[i, dim:, :] = jnp.ones_like(values_t[i, dim:, :])

    gate_copy.wait()
    picked = lax.broadcasted_iota(jnp.int32, (gate_all.shape[0], dim), 0) == step[0]
    for i in range(heads):
        cols = pl.ds(pl.multiple_of(a * width + i * dim, dim), dim)
        gate_row[i] = jnp.sum(
            jnp.where(picked, gate_all[:, cols].astype(F32), 0.0), axis=0, keepdims=True
        )

    def attend(r, i):
        q = q_all[r, i].reshape(2 * block, dim)
        scores = lax.dot_general(
            keys[i], q, (((1,), (1,)), ((), ())), preferred_element_type=F32
        )
        weights = jnp.exp(scores * (dim ** (-0.5))).astype(BF16)
        part[r, i] = jnp.dot(values_t[i], weights, preferred_element_type=F32)

    def partial_sum(r, i, d):
        return part[r, i, :, d * block : (d + 1) * block]

    def back_copy(r, i, d):
        far = r == reach
        if far:
            d = far_way(i)
        return pltpu.make_async_remote_copy(
            src_ref=send.at[0, i, 1] if far else send.at[r, i, d],
            dst_ref=back.at[r - 1, i, d],
            send_sem=back_send.at[r, i, 0 if far else d],
            recv_sem=back_recv.at[r - 1, i, d],
            device_id=(sec, ring_step(1 - d)),
            device_id_type=MESH,
        )

    def back_arrived(r, i, d):
        pltpu.make_async_remote_copy(
            src_ref=back.at[r, i, d],
            dst_ref=back.at[r, i, d],
            send_sem=back_send.at[0, i, 0],
            recv_sem=back_recv.at[r, i, d],
            device_id=(sec, up),
            device_id_type=MESH,
        ).wait_recv()

    for r in range(1, reach):

        def forward(i, carry, r=r):
            for d in range(2):
                turn_arrived(r, i, d)
                if r + 1 < reach:
                    turn(r, i, d).start()
            if r + 1 == reach:
                turn(r, i, far_way(i)).start()
            return carry

        lax.fori_loop(0, heads, forward, 0)
        if r == 1:
            own_v.wait()
            own_h.wait()
            for kind in (1, 2):
                for d in range(1, groups):
                    first_arrived(kind, d)
            for i in range(heads):
                values_t[i, 0:dim, stale_keys:] = v_in[:, i * dim : (i + 1) * dim].T

        def work(i, carry, r=r):
            attend(r, i)
            if r + 1 == reach:
                for d in range(2):

                    @pl.when(far_way(i) != d)
                    def _(d=d):
                        send[r, i, d] = partial_sum(r, i, d).astype(BF16)
                        back_copy(r, i, d).start()

            return carry

        lax.fori_loop(0, heads, work, 0)

    def far_work(i, carry):
        turn_arrived(reach, i, 0)
        attend(0, i)
        send[0, i, 1] = partial_sum(0, i, 1).astype(BF16)
        back_copy(reach, i, 0).start()
        return carry

    lax.fori_loop(0, heads, far_work, 0)

    for r in range(reach - 1, 0, -1):

        def add_on(i, carry, r=r):
            for d in range(2):

                def go(d=d):
                    back_arrived(r, i, d)
                    send[r, i, d] = (
                        partial_sum(r, i, d) + back[r, i, d].astype(F32)
                    ).astype(BF16)
                    back_copy(r, i, d).start()

                if r + 1 == reach:
                    pl.when(far_way(i) == d)(go)
                else:
                    go()
            return carry

        lax.fori_loop(0, heads, add_on, 0)

    for d in range(1, groups):
        first_arrived(3, d)

    def out_copy(i, d):
        to = lax.rem(a + d, groups)
        rows = pl.ds(pl.multiple_of(to * toks, toks), toks)
        cols = pl.ds(pl.multiple_of(a * width + i * dim, dim), dim)
        return pltpu.make_async_remote_copy(
            src_ref=mixed.at[i, rows, :],
            dst_ref=out.at[0, :, cols],
            send_sem=out_send.at[i, d],
            recv_sem=out_recv.at[i, d],
            device_id=(next_sec, peer(d)),
            device_id_type=MESH,
        )

    def out_arrived(i, d):
        source = lax.rem(a + groups - d, groups)
        cols = pl.ds(pl.multiple_of(source * width + i * dim, dim), dim)
        pltpu.make_async_remote_copy(
            src_ref=mixed.at[0, pl.ds(0, toks), :],
            dst_ref=out.at[0, :, cols],
            send_sem=out_send.at[i, d],
            recv_sem=out_recv.at[i, d],
            device_id=(next_sec, peer(d)),
            device_id_type=MESH,
        ).wait_recv()

    for i in range(heads):
        for d in range(2):
            back_arrived(0, i, d)
        total = partial_sum(0, i, 0) + back[0, i, 0].astype(F32) + back[0, i, 1].astype(F32)
        attention = (total[0:dim] / total[dim : dim + 1]).T
        attention = attention.astype(BF16).astype(F32)
        mixed[i] = (
            h_in[:, i * dim : (i + 1) * dim].astype(F32) + gate_row[i] * attention
        ).astype(BF16)
        for d in range(groups):
            out_copy(i, d).start()

    for kind in range(4):
        for d in range(1, groups):
            first_copy(kind, d).wait_send()

    def sent(i, carry):
        for r in range(reach):
            if r + 1 < reach:
                for d in range(2):
                    turn(r, i, d).wait_send()
            else:
                turn(r, i, far_way(i)).wait_send()
        for r in range(1, reach):
            for d in range(2):
                back_copy(r, i, d).wait_send()
        back_copy(reach, i, 0).wait_send()
        return carry

    lax.fori_loop(0, heads, sent, 0)
    for i in range(heads):
        for d in range(groups):
            out_copy(i, d).wait_send()
            out_arrived(i, d)


def shards(sections, fresh_qkv, stale_cache, norm_gains, hidden, gate_table, patch_index, step_index):
    seq_count = lax.axis_size("seq")
    groups = HEAD_GROUPS
    toks, full = hidden.shape[1:]
    width = full // groups
    heads = width // HEAD_DIM
    dim = HEAD_DIM
    block = toks * groups
    reach = seq_count // groups // 2
    patches, stale_rows = stale_cache.shape[2:4]
    key_count = (patches - 1) * stale_rows + block
    tall = dim + 16
    fresh = fresh_qkv.transpose(0, 2, 1, 3)
    anywhere = pl.BlockSpec(memory_space=pl.ANY)
    vmem = pl.BlockSpec(memory_space=pltpu.VMEM)
    smem = pl.BlockSpec(memory_space=pltpu.SMEM)
    dma = pltpu.SemaphoreType.DMA
    return pl.pallas_call(
        functools.partial(kernel, sections, seq_count),
        out_shape=jax.ShapeDtypeStruct(hidden.shape, BF16),
        in_specs=[anywhere, anywhere, vmem, anywhere, anywhere, smem, smem],
        out_specs=anywhere,
        scratch_shapes=[
            pltpu.VMEM((2, toks, full), BF16),
            pltpu.VMEM((patches, stale_rows, 2 * width), BF16),
            pltpu.VMEM(gate_table.shape[1:], BF16),
            pltpu.VMEM((heads, 1, dim), F32),
            pltpu.VMEM((groups, heads, toks, dim), BF16),
            pltpu.VMEM((groups, heads, toks, dim), BF16),
            pltpu.VMEM((reach, heads, 2, block, dim), BF16),
            pltpu.VMEM((heads, key_count, dim), BF16),
            pltpu.VMEM((heads, tall, key_count), BF16),
            pltpu.VMEM((block, width), BF16),
            pltpu.VMEM((block, width), BF16),
            pltpu.VMEM((reach, heads, tall, 2 * block), F32),
            pltpu.VMEM((reach, heads, 2, tall, block), BF16),
            pltpu.VMEM((reach, heads, 2, tall, block), BF16),
            pltpu.VMEM((heads, block, dim), BF16),
            dma((3,)),
            dma((2,)),
            dma((4, groups)),
            dma((4, groups)),
            dma((reach, heads, 2)),
            dma((reach + 1, heads, 2)),
            dma((reach + 1, heads, 2)),
            dma((reach, heads, 2)),
            dma((heads, groups)),
            dma((heads, groups)),
        ],
        compiler_params=pltpu.CompilerParams(
            collective_id=0, has_side_effects=True, vmem_limit_bytes=32 * 1024 * 1024
        ),
    )(fresh, stale_cache, norm_gains, hidden, gate_table, patch_index, step_index)


def solution(mesh):
    return jax.shard_map(
        functools.partial(shards, mesh.shape["section"]),
        mesh=mesh,
        in_specs=(
            P("section", "seq", None, None),
            P("section", "seq", None, None, None),
            P("section", None, None),
            P("section", "seq", None),
            P("section", None, None),
            P("section"),
            P("section"),
        ),
        out_specs=P("section", "seq", None),
        check_vma=False,
    )
```

time: 161 us -> 66.2 us (0.41)
  the two profiles are of different devices: /device:TPU:1 before, /device:TPU:67 now
where the time goes in v1:
time: 66.2 us; the launch traced here: 66 us
  Pallas kernels  59.4 us (90%)
  local copies, waits for them, and re-layouts  5.28 us (8%)
  between operations  1.32 us (2%)
    pallas_call x1, Pallas kernels, shards(): pl.pallas_call(functools.partial(kernel, sections, seq_count), out_shape=...  59.4 us
    unnamed x11, local copies, waits for them, and re-layouts  5.28 us

profile of v1, /device:TPU:67, one launch (start us, length us, event | category | flops | bytes accessed | tf_op | source)
XLA Modules:
  0.0 66.0 jit_solution(10901861084352912383)
XLA Ops:
  1.3 0.0 copy-start.4
  1.3 0.7 %copy-done.4 = f32[1,2,128]{2,1,0:T(2,128)S(1)} copy-done((f32[1,2,128]{2,1,0:T(2,128)S(1)}, f32[1,2,128]{2,1,0:T(2,128)}, u32[]{:S(2)}) %copy-start.4) | copy-done | bytes 1048
  2.0 0.0 copy-start
  2.0 1.1 %copy-done = bf16[1,1,4,128,768]{4,3,2,1,0:T(8,128)(2,1)S(1)} copy-done((bf16[1,1,4,128,768]{4,3,2,1,0:T(8,128)(2,1)S(1)}, bf16[1,1,4,128,768]{4,3,2,1,0:T(8,128)(2,1)}, u32[]{:S(2)}) %copy-start) | copy-done | bytes 786456
  3.1 0.0 copy-start.1
  3.1 1.0 %copy-done.1 = bf16[1,50,3072]{2,1,0:T(8,128)(2,1)S(1)} copy-done((bf16[1,50,3072]{2,1,0:T(8,128)(2,1)S(1)}, bf16[1,50,3072]{2,1,0:T(8,128)(2,1)}, u32[]{:S(2)}) %copy-start.1) | copy-done | bytes 307224
  4.1 0.0 copy-start.2
  4.1 1.0 %copy-done.2 = bf16[1,16,3,3072]{3,1,2,0:T(8,128)(2,1)S(1)} copy-done((bf16[1,16,3,3072]{3,1,2,0:T(8,128)(2,1)S(1)}, bf16[1,16,3,3072]{3,1,2,0:T(8,128)(2,1)}, u32[]{:S(2)}) %copy-start.2) | copy-done | bytes 294936
  5.1 0.0 copy-start.3
  5.1 0.9 %copy-done.3 = bf16[1,16,3072]{2,1,0:T(8,128)(2,1)S(1)} copy-done((bf16[1,16,3072]{2,1,0:T(8,128)(2,1)S(1)}, bf16[1,16,3072]{2,1,0:T(8,128)(2,1)}, u32[]{:S(2)}) %copy-start.3) | copy-done | bytes 98328
  5.9 59.4 %shard_map.73 = bf16[1,16,3072]{2,1,0:T(8,128)(2,1)S(1)} custom-call(bf16[1,3,16,3072]{3,2,1,0:T(8,128)(2,1)S(1)} %bitcast.1, bf16[1,1,4,128,768]{4,3,2,1,0:T(8,128)(2,1)S(1)} %copy-done, f32[1,2,128]{2,1,0:T(2,128)S(1)} %copy-done.4, bf16[1,16,3072]{2,1,0:T(8,128)(2,1)S(1)} %copy-done.3, bf16[1,50,3072]{2,1,0:T(8,128)(2,1)S(1)} %copy-done.1, ...), custom_call_target="tpu_custom_call" | custom-call | tf_op jit(solution)/shard_map/pallas_call | solution.py:399
  65.3 0.6 copy.11
Async XLA Ops:
  1.3 0.7 %copy-start.4 = (f32[1,2,128]{2,1,0:T(2,128)S(1)}, f32[1,2,128]{2,1,0:T(2,128)}, u32[]{:S(2)}) copy-start(f32[1,2,128]{2,1,0:T(2,128)} %gains.1) | copy-start | bytes 3076
  2.0 1.1 %copy-start = (bf16[1,1,4,128,768]{4,3,2,1,0:T(8,128)(2,1)S(1)}, bf16[1,1,4,128,768]{4,3,2,1,0:T(8,128)(2,1)}, u32[]{:S(2)}) copy-start(bf16[1,1,4,128,768]{4,3,2,1,0:T(8,128)(2,1)} %stale.1) | copy-start | bytes 2359300
  3.1 1.0 %copy-start.1 = (bf16[1,50,3072]{2,1,0:T(8,128)(2,1)S(1)}, bf16[1,50,3072]{2,1,0:T(8,128)(2,1)}, u32[]{:S(2)}) copy-start(bf16[1,50,3072]{2,1,0:T(8,128)(2,1)} %gate.1) | copy-start | bytes 921604
  4.1 1.0 %copy-start.2 = (bf16[1,16,3,3072]{3,1,2,0:T(8,128)(2,1)S(1)}, bf16[1,16,3,3072]{3,1,2,0:T(8,128)(2,1)}, u32[]{:S(2)}) copy-start(bf16[1,16,3,3072]{3,1,2,0:T(8,128)(2,1)} %param.7) | copy-start | bytes 884740
  5.1 0.9 %copy-start.3 = (bf16[1,16,3072]{2,1,0:T(8,128)(2,1)S(1)}, bf16[1,16,3072]{2,1,0:T(8,128)(2,1)}, u32[]{:S(2)}) copy-start(bf16[1,16,3072]{2,1,0:T(8,128)(2,1)} %hidden.1) | copy-start | bytes 294916

commit v2 on v1

v2 whole, which is shorter than its diff:
```python
import functools

import jax
import jax.numpy as jnp
from jax import lax
from jax.experimental import pallas as pl
from jax.experimental.pallas import tpu as pltpu
from jax.sharding import PartitionSpec as P

HEADS = 24
HEAD_DIM = 128
HEAD_GROUPS = 8
SPACING = 4
MESH = pl.DeviceIdType.MESH
F32 = jnp.float32
BF16 = jnp.bfloat16


def slot_pair(r):
    if r == 0:
        return 0
    if r == SPACING:
        return 1
    return 2 * r if r > 0 else 1 - 2 * r


def kernel(
    sections,
    seq_count,
    fresh,
    stale,
    gains_in,
    hidden,
    gate,
    patch,
    step,
    out,
    raw,
    old,
    gains,
    gate_cols,
    gate_row,
    q_out,
    k_out,
    q_home,
    v_in,
    h_in,
    k_mine,
    v_mine,
    k_new,
    v_new,
    q_site,
    k_site,
    v_site,
    part,
    send,
    back,
    mixed,
    local_sem,
    first_send,
    first_recv,
    kv_send,
    kv_recv,
    q_send,
    q_recv,
    back_send,
    back_recv,
    out_send,
    out_recv,
):
    groups = HEAD_GROUPS
    ring = seq_count // groups
    heads = q_out.shape[1]
    toks = q_out.shape[2]
    dim = HEAD_DIM
    width = heads * dim
    block = groups * toks
    rows = old.shape[1]
    kept = old.shape[0] - 1
    stale_keys = kept * rows
    stale_at = (0, stale_keys, 2 * stale_keys, 3 * stale_keys, 3 * stale_keys + (kept - 1) * rows)
    fresh_base = 4 * stale_keys
    fresh_at = tuple(fresh_base + n * block for n in range(4))

    sec = lax.axis_index("section")
    me = lax.axis_index("seq")
    y = me // groups
    a = me % groups
    next_sec = lax.rem(sec + 1, sections)
    prev_sec = lax.rem(sec + sections - 1, sections)
    duty = lax.rem(y + SPACING - 2 * lax.rem(a, 2), SPACING)
    on_duty = duty < heads

    def peer(d):
        return y * groups + lax.rem(a + d, groups)

    def along(r):
        return lax.rem(y + ring + r, ring) * groups + a

    loads = [
        pltpu.make_async_copy(src, dst, local_sem.at[n])
        for n, (src, dst) in enumerate(
            (
                (gains_in.at[0], gains),
                (fresh.at[0, 0], raw.at[0]),
                (fresh.at[0, 1], raw.at[1]),
                (stale.at[0, 0], old),
            )
        )
    ]
    for load in loads:
        load.start()
    got_gains, got_q, got_k, got_old = loads

    barrier = pltpu.get_barrier_semaphore()
    for d in range(1, groups):
        pl.semaphore_signal(barrier, inc=1, device_id=(sec, peer(d)), device_id_type=MESH)
    for r in range(1, ring):
        pl.semaphore_signal(barrier, inc=1, device_id=(sec, along(r)), device_id_type=MESH)
    for d in range(groups):
        pl.semaphore_signal(barrier, inc=1, device_id=(prev_sec, peer(d)), device_id_type=MESH)

    mine = pl.ds(pl.multiple_of(a * toks, toks), toks)
    my_cols = pl.ds(pl.multiple_of(a * width, dim), width)
    late_loads = [
        pltpu.make_async_copy(src, dst, local_sem.at[len(loads) + n])
        for n, (src, dst) in enumerate(
            (
                (fresh.at[0, 2, :, my_cols], v_in.at[mine]),
                (hidden.at[0, :, my_cols], h_in.at[mine]),
                (gate.at[0, :, my_cols], gate_cols),
            )
        )
    ]
    for load in late_loads:
        load.start()

    def norm(which, stage):
        gain = gains[which : which + 1, :]
        for g in range(groups):
            for i in range(heads):
                col = (g * heads + i) * dim
                x = raw[which, :, col : col + dim].astype(F32)
                factor = lax.rsqrt(jnp.mean(x * x, axis=-1, keepdims=True) + 1e-06)
                stage[g, i] = (x * factor * gain).astype(BF16)

    got_gains.wait()
    got_q.wait()
    norm(0, q_out)
    q_home[:, mine, :] = q_out[a]

    pl.semaphore_wait(barrier, 2 * groups + ring - 2)

    def first_copy(kind, d):
        to = lax.rem(a + d, groups)
        cols = pl.ds(pl.multiple_of(to * width, dim), width)
        src, dst = (
            (lambda: q_out.at[to], lambda: q_home.at[:, mine, :]),
            (lambda: k_out.at[to], lambda: k_new.at[:, mine, :]),
            (lambda: fresh.at[0, 2, :, cols], lambda: v_in.at[mine]),
            (lambda: hidden.at[0, :, cols], lambda: h_in.at[mine]),
        )[kind]
        return pltpu.make_async_remote_copy(
            src_ref=src(),
            dst_ref=dst(),
            send_sem=first_send.at[kind, d],
            recv_sem=first_recv.at[kind, d],
            device_id=(sec, peer(d)),
            device_id_type=MESH,
        )

    def arrived(dst, sem):
        pltpu.make_async_remote_copy(
            src_ref=dst,
            dst_ref=dst,
            send_sem=first_send.at[0, 0],
            recv_sem=sem,
            device_id=(sec, peer(1)),
            device_id_type=MESH,
        ).wait_recv()

    def first_arrived(kind, d):
        source = lax.rem(a + groups - d, groups)
        spot = pl.ds(pl.multiple_of(source * toks, toks), toks)
        dst = (
            lambda: q_home.at[:, spot, :],
            lambda: k_new.at[:, spot, :],
            lambda: v_in.at[spot],
            lambda: h_in.at[spot],
        )[kind]()
        arrived(dst, first_recv.at[kind, d])

    for d in range(1, groups):
        first_copy(0, d).start()
    got_k.wait()
    norm(1, k_out)
    for kind in (1, 2):
        for d in range(1, groups):
            first_copy(kind, d).start()
    k_new[:, mine, :] = k_out[a]

    got_old.wait()
    skip = patch[0]
    for n in range(kept):
        m = n + (n >= skip).astype(jnp.int32)
        spot = slice(n * rows, (n + 1) * rows)
        for i in range(heads):
            k_mine[i, spot, :] = old[m, :, i * dim : (i + 1) * dim]
            v_mine[i, :, spot] = old[m, :, width + i * dim : width + (i + 1) * dim].T

    routes = (
        (1, 1, 0, kept, 1, True),
        (3, -1, 0, kept, 2, True),
        (2, 2, 0, kept - 1, 3, False),
        (2, -2, kept - 1, kept, 4, True),
    )
    fresh_number = {1: 1, 2: 2, 4: 3}

    def kv_copies(route, kinds):
        case, places, low, high, number, with_fresh = routes[route]
        i = lax.rem(duty + case, SPACING)
        count = (high - low) * rows
        spot, at = pl.ds(low * rows, count), pl.ds(stale_at[number], count)
        pairs = [
            (k_mine.at[i, spot, :], k_site.at[at, :]),
            (v_mine.at[i, :, spot], v_site.at[pl.ds(0, dim), at]),
        ]
        if with_fresh:
            at = pl.ds(fresh_at[fresh_number[number]], block)
            pairs += [
                (k_new.at[i], k_site.at[at, :]),
                (v_new.at[i], v_site.at[pl.ds(0, dim), at]),
            ]
        return [
            pltpu.make_async_remote_copy(
                src_ref=pairs[kind][0],
                dst_ref=pairs[kind][1],
                send_sem=kv_send.at[route, kind],
                recv_sem=kv_recv.at[route, kind],
                device_id=(sec, along(places)),
                device_id_type=MESH,
            )
            for kind in kinds
            if kind < len(pairs)
        ]

    def kv_start(kinds):
        for route in range(len(routes)):

            @pl.when(lax.rem(duty + routes[route][0], SPACING) < heads)
            def _(route=route):
                for copy in kv_copies(route, kinds):
                    copy.start()

    kv_start((0, 1))

    def q_copy(i, k):
        case = lax.rem(i - duty + SPACING, SPACING)
        places = case - k * SPACING
        if k == 0:
            slot = 2 * case + jnp.where(case == 0, 0, 1)
        else:
            slot = jnp.where(case == 0, 1, 2 * (SPACING - case))
        return case, pltpu.make_async_remote_copy(
            src_ref=q_home.at[i],
            dst_ref=q_site.at[slot],
            send_sem=q_send.at[i, k],
            recv_sem=q_recv.at[slot],
            device_id=(sec, along(places)),
            device_id_type=MESH,
        )

    for d in range(1, groups):
        first_arrived(0, d)
    for k in (1, 0):
        for i in range(heads):
            case, copy = q_copy(i, k)
            if k == 0:
                pl.when(case != 0)(copy.start)
            else:
                copy.start()

    for d in range(1, groups):
        first_copy(3, d).start()

    @pl.when(on_duty)
    def _():
        q_site[0] = q_home[duty]
        k_site[0:stale_keys, :] = k_mine[duty]
        v_site[0:dim, 0:stale_keys] = v_mine[duty]
        v_site[dim:, :] = jnp.ones_like(v_site[dim:, :])

    late_loads[0].wait()
    for kind in (1, 2):
        for d in range(1, groups):
            first_arrived(kind, d)
    for i in range(heads):
        v_new[i] = v_in[:, i * dim : (i + 1) * dim].T
    kv_start((2, 3))

    late_loads[2].wait()
    picked = lax.broadcasted_iota(jnp.int32, gate_cols.shape, 0) == step[0]
    gate_row[...] = jnp.sum(
        jnp.where(picked, gate_cols[...].astype(F32), 0.0), axis=0, keepdims=True
    )

    def attend(p, low, high):
        q = q_site[2 * p : 2 * p + 2].reshape(2 * block, dim)
        scores = lax.dot_general(
            k_site[low:high, :], q, (((1,), (1,)), ((), ())), preferred_element_type=F32
        )
        weights = jnp.exp(scores * (dim ** (-0.5))).astype(BF16)
        return jnp.dot(v_site[:, low:high], weights, preferred_element_type=F32)

    def back_copy(r):
        k = 0 if (-r) % ring < SPACING else 1
        return pltpu.make_async_remote_copy(
            src_ref=send.at[slot_pair(r)],
            dst_ref=back.at[duty, k],
            send_sem=back_send.at[slot_pair(r)],
            recv_sem=back_recv.at[duty, k],
            device_id=(sec, along(r)),
            device_id_type=MESH,
        )

    pairs = ((0, SPACING), (1, -1), (2, -2), (3, -3))

    @pl.when(on_duty)
    def _():
        for route in range(len(routes)):
            number, count = routes[route][4], (routes[route][3] - routes[route][2]) * rows
            at = pl.ds(stale_at[number], count)
            arrived(k_site.at[at, :], kv_recv.at[route, 0])
            arrived(v_site.at[pl.ds(0, dim), at], kv_recv.at[route, 1])
        for p in (1, 2, 3, 0):
            for r in pairs[p]:
                if r:
                    slot = slot_pair(r)
                    arrived(q_site.at[slot], q_recv.at[slot])
            part[p] = attend(p, 0, fresh_base)
        at = pl.ds(fresh_base, block)
        k_site[at, :] = k_new[duty]
        v_site[pl.ds(0, dim), at] = v_new[duty]
        for route in range(len(routes)):
            if routes[route][5]:
                at = pl.ds(fresh_at[fresh_number[routes[route][4]]], block)
                arrived(k_site.at[at, :], kv_recv.at[route, 2])
                arrived(v_site.at[pl.ds(0, dim), at], kv_recv.at[route, 3])
        for p in (0, 3, 2, 1):
            total = part[p] + attend(p, fresh_base, k_site.shape[0])
            for n, r in enumerate(pairs[p]):
                piece = total[:, n * block : (n + 1) * block].astype(BF16)
                if r == 0:
                    back[duty, 0] = piece
                else:
                    send[slot_pair(r)] = piece
                    back_copy(r).start()

    late_loads[1].wait()
    for d in range(1, groups):
        first_arrived(3, d)

    def out_copy(i, d):
        to = lax.rem(a + d, groups)
        spot = pl.ds(pl.multiple_of(to * toks, toks), toks)
        cols = pl.ds(pl.multiple_of(a * width + i * dim, dim), dim)
        return pltpu.make_async_remote_copy(
            src_ref=mixed.at[i, spot, :],
            dst_ref=out.at[0, :, cols],
            send_sem=out_send.at[i, d],
            recv_sem=out_recv.at[i, d],
            device_id=(next_sec, peer(d)),
            device_id_type=MESH,
        )

    for i in range(heads):
        case = lax.rem(i - duty + SPACING, SPACING)

        @pl.when(case != 0)
        def _(i=i):
            arrived(back.at[i, 0], back_recv.at[i, 0])

        arrived(back.at[i, 1], back_recv.at[i, 1])
        total = back[i, 0].astype(F32) + back[i, 1].astype(F32)
        attention = (total[0:dim] / total[dim : dim + 1]).T
        attention = attention.astype(BF16).astype(F32)
        cols = slice(i * dim, (i + 1) * dim)
        mixed[i] = (h_in[:, cols].astype(F32) + gate_row[:, cols] * attention).astype(BF16)
        for d in range(groups):
            out_copy(i, d).start()

    for kind in range(4):
        for d in range(1, groups):
            first_copy(kind, d).wait_send()
    for route in range(len(routes)):

        @pl.when(lax.rem(duty + routes[route][0], SPACING) < heads)
        def _(route=route):
            for copy in kv_copies(route, (0, 1, 2, 3)):
                copy.wait_send()

    for i in range(heads):
        for k in range(2):
            case, copy = q_copy(i, k)
            if k == 0:
                pl.when(case != 0)(copy.wait_send)
            else:
                copy.wait_send()

    @pl.when(on_duty)
    def _():
        for pair in pairs:
            for r in pair:
                if r:
                    back_copy(r).wait_send()

    for i in range(heads):
        for d in range(groups):
            out_copy(i, d).wait_send()
            source = lax.rem(a + groups - d, groups)
            cols = pl.ds(pl.multiple_of(source * width + i * dim, dim), dim)
            arrived(out.at[0, :, cols], out_recv.at[i, d])


def shards(sections, fresh_qkv, stale_cache, norm_gains, hidden, gate_table, patch_index, step_index):
    seq_count = lax.axis_size("seq")
    groups = HEAD_GROUPS
    ring = seq_count // groups
    toks, full = hidden.shape[1:]
    width = full // groups
    heads = width // HEAD_DIM
    dim = HEAD_DIM
    block = toks * groups
    patches, rows = stale_cache.shape[2:4]
    stale_keys = (patches - 1) * rows
    site_keys = 4 * (stale_keys + block)
    tall = dim + 16
    fresh = fresh_qkv.transpose(0, 2, 1, 3)
    hbm = pl.BlockSpec(memory_space=pltpu.HBM)
    smem = pl.BlockSpec(memory_space=pltpu.SMEM)
    dma = pltpu.SemaphoreType.DMA
    return pl.pallas_call(
        functools.partial(kernel, sections, seq_count),
        out_shape=jax.ShapeDtypeStruct(hidden.shape, BF16),
        in_specs=[hbm] * 5 + [smem] * 2,
        out_specs=pl.BlockSpec(memory_space=pl.ANY),
        scratch_shapes=[
            pltpu.VMEM((2, toks, full), BF16),
            pltpu.VMEM((patches, rows, 2 * width), BF16),
            pltpu.VMEM((2, dim), F32),
            pltpu.VMEM((gate_table.shape[1], width), BF16),
            pltpu.VMEM((1, width), F32),
            pltpu.VMEM((groups, heads, toks, dim), BF16),
            pltpu.VMEM((groups, heads, toks, dim), BF16),
            pltpu.VMEM((heads, block, dim), BF16),
            pltpu.VMEM((block, width), BF16),
            pltpu.VMEM((block, width), BF16),
            pltpu.VMEM((heads, stale_keys, dim), BF16),
            pltpu.VMEM((heads, dim, stale_keys), BF16),
            pltpu.VMEM((heads, block, dim), BF16),
            pltpu.VMEM((heads, dim, block), BF16),
            pltpu.VMEM((ring, block, dim), BF16),
            pltpu.VMEM((site_keys, dim), BF16),
            pltpu.VMEM((tall, site_keys), BF16),
            pltpu.VMEM((ring // 2, tall, 2 * block), F32),
            pltpu.VMEM((ring, tall, block), BF16),
            pltpu.VMEM((heads, 2, tall, block), BF16),
            pltpu.VMEM((heads, block, dim), BF16),
            dma((7,)),
            dma((4, groups)),
            dma((4, groups)),
            dma((4, 4)),
            dma((4, 4)),
            dma((heads, 2)),
            dma((ring,)),
            dma((ring,)),
            dma((heads, 2)),
            dma((heads, groups)),
            dma((heads, groups)),
        ],
        compiler_params=pltpu.CompilerParams(
            collective_id=0, has_side_effects=True, vmem_limit_bytes=24 * 1024 * 1024
        ),
    )(
        *(
            pltpu.with_memory_space_constraint(array, pltpu.HBM)
            for array in (
                fresh,
                stale_cache,
                norm_gains,
                hidden,
                gate_table,
            )
        ),
        patch_index,
        step_index,
    )


def solution(mesh):
    return jax.shard_map(
        functools.partial(shards, mesh.shape["section"]),
        mesh=mesh,
        in_specs=(
            P("section", "seq", None, None),
            P("section", "seq", None, None, None),
            P("section", None, None),
            P("section", "seq", None),
            P("section", None, None),
            P("section"),
            P("section"),
        ),
        out_specs=P("section", "seq", None),
        check_vma=False,
    )
```

time: 66.2 us -> 50.7 us (0.77)
  the two profiles are of different devices: /device:TPU:67 before, /device:TPU:1 now
where the time goes in v2:
time: 50.7 us; the launch traced here: 50.6 us
  Pallas kernels  48.7 us (96%)
  between operations  1.3 us (3%)
  local copies, waits for them, and re-layouts  0.64 us (1%)
    pallas_call x1, Pallas kernels, shards(): pl.pallas_call(functools.partial(kernel, sections, seq_count), out_shape=...  48.7 us

profile of v2, /device:TPU:1, one launch (start us, length us, event | category | flops | bytes accessed | tf_op | source)
XLA Modules:
  0.0 50.6 jit_solution(15954463775478512045)
XLA Ops:
  1.3 48.7 %shard_map.73 = bf16[1,16,3072]{2,1,0:T(8,128)(2,1)S(1)} custom-call(bf16[1,3,16,3072]{3,2,1,0:T(8,128)(2,1)} %bitcast.1, bf16[1,1,4,128,768]{4,3,2,1,0:T(8,128)(2,1)} %stale.1, f32[1,2,128]{2,1,0:T(2,128)} %gains_in.1, bf16[1,16,3072]{2,1,0:T(8,128)(2,1)} %hidden.1, bf16[1,50,3072]{2,1,0:T(8,128)(2,1)} %gate.1, s32[1]{0:T(128)S(6)} %copy.9.patch, ...), custom_call_target="tpu_custom_call" | custom-call | tf_op jit(solution)/shard_map/pallas_call | solution.py:442
  50.0 0.6 %copy.11 = bf16[1,16,3072]{2,1,0:T(8,128)(2,1)} copy(bf16[1,16,3072]{2,1,0:T(8,128)(2,1)S(1)} %shard_map.73) | data formatting | bytes 196608

commit v3 on v2

v3 whole, which is shorter than its diff:
```python
import functools

import jax
import jax.numpy as jnp
from jax import lax
from jax.experimental import pallas as pl
from jax.experimental.pallas import tpu as pltpu
from jax.sharding import PartitionSpec as P

HEADS = 24
HEAD_DIM = 128
HEAD_GROUPS = 8
SITES = 4
MESH = pl.DeviceIdType.MESH
F32 = jnp.float32
BF16 = jnp.bfloat16


def slot_of(r):
    if r == 0:
        return 0
    if r == SITES:
        return 1
    return 2 * r if r > 0 else 1 - 2 * r


PLACES = ((0, 2, -2, 4), (1, -1, 3, -3))


def kernel(
    sections,
    seq_count,
    fresh,
    stale,
    gains_in,
    hidden,
    gate,
    patch,
    step,
    out,
    raw,
    old,
    gains,
    gate_cols,
    gate_row,
    q_out,
    kv_out,
    q_home,
    h_in,
    k_mine,
    v_mine,
    q_site,
    k_site,
    v_site,
    kv_new,
    send,
    back,
    mixed,
    local_sem,
    first_send,
    first_recv,
    new_send,
    new_recv,
    kv_send,
    kv_recv,
    q_send,
    q_recv,
    back_send,
    back_recv,
    out_send,
    out_recv,
):
    groups = HEAD_GROUPS
    ring = seq_count // groups
    heads = q_out.shape[1]
    toks = q_out.shape[2]
    dim = HEAD_DIM
    width = heads * dim
    block = groups * toks
    rows = old.shape[1]
    kept = old.shape[0] - 1
    stale_keys = kept * rows
    last = (kept - 1) * rows
    before_at, after_at, fresh_at = stale_keys, stale_keys + last, 2 * stale_keys

    sec = lax.axis_index("section")
    me = lax.axis_index("seq")
    y = me // groups
    a = me % groups
    next_sec = lax.rem(sec + 1, sections)
    prev_sec = lax.rem(sec + sections - 1, sections)
    core = lax.rem(a, 2)
    parity = lax.rem(y, 2)

    def duty_of(parity, core):
        count = 1 + jnp.where(parity == core, 1, 0)
        return parity * (heads - count), count

    first_head, duty_count = duty_of(parity, core)

    def away(i, core=core):
        return lax.rem((i + core) // 2 + parity, 2)

    def flipped(d):
        bits = [1 << n for n in range(groups.bit_length() - 1)]
        return sum(
            bit * (1 - lax.rem(a // bit, 2) if d & bit else lax.rem(a // bit, 2)) for bit in bits
        )

    def along(r, d=0):
        return lax.rem(y + ring + r, ring) * groups + flipped(d)

    def peer(d):
        return along(0, d)

    pair, side = a // 2, a // (groups // 2)
    pieces = [
        pl.ds(pl.multiple_of(start * toks, toks), count * toks)
        for start, count in (
            (2 * pair, 2),
            (2 * (pair + 1 - 2 * lax.rem(pair, 2)), 2),
            ((1 - side) * (groups // 2), groups // 2),
        )
    ]

    barrier = pltpu.get_barrier_semaphore()

    def greet(section, seq):
        pl.semaphore_signal(barrier, inc=1, device_id=(section, seq), device_id_type=MESH)

    for d in range(groups - 1, 0, -1):
        greet(sec, along(0, d))
    for d in range(groups - 1, -1, -1):
        greet(sec, along(1, d))
    for r in (4, 3, -3, 2, -2, -1):
        greet(sec, along(r))
    greet(prev_sec, me)
    greeted = 2 * groups + 6

    mine = pl.ds(pl.multiple_of(a * toks, toks), toks)
    my_cols = pl.ds(pl.multiple_of(a * width, dim), width)
    loads = [
        pltpu.make_async_copy(src, dst, local_sem.at[n])
        for n, (src, dst) in enumerate(
            (
                (gains_in.at[0], gains),
                (fresh.at[0], raw),
                (stale.at[0, 0], old),
                (hidden.at[0, :, my_cols], h_in.at[mine]),
                (gate.at[0, :, my_cols], gate_cols),
            )
        )
    ]
    got_gains, got_raw, got_old, got_h, got_gate = loads
    for load in loads:
        load.start()

    def normed(which, g, i):
        col = (g * heads + i) * dim
        x = raw[which, :, col : col + dim].astype(F32)
        factor = lax.rsqrt(jnp.mean(x * x, axis=-1, keepdims=True) + 1e-06)
        return (x * factor * gains[which : which + 1, :]).astype(BF16)

    got_gains.wait()
    got_raw.wait()
    for g in range(groups):
        for i in range(heads):
            q_out[g, i] = normed(0, g, i)
    for g in range(groups):
        for i in range(heads):
            col = (g * heads + i) * dim
            kv_out[g, i, 0] = normed(1, g, i)
            kv_out[g, i, 1] = raw[2, :, col : col + dim]
    q_home[:, mine, :] = q_out[a]

    got_old.wait()
    skip = patch[0]
    for n in range(kept):
        m = n + (n >= skip).astype(jnp.int32)
        spot = slice(n * rows, (n + 1) * rows)
        for i in range(heads):
            k_mine[i, spot, :] = old[m, :, i * dim : (i + 1) * dim]
            v_mine[i, :, spot] = old[m, :, width + i * dim : width + (i + 1) * dim].T

    pl.semaphore_wait(barrier, greeted)

    def first_copy(kind, d):
        to = flipped(d)
        cols = pl.ds(pl.multiple_of(to * width, dim), width)
        src, dst = (
            (lambda: q_out.at[to], lambda: q_home.at[:, mine, :]),
            (lambda: hidden.at[0, :, cols], lambda: h_in.at[mine]),
        )[kind]
        return pltpu.make_async_remote_copy(
            src_ref=src(),
            dst_ref=dst(),
            send_sem=first_send.at[kind, d],
            recv_sem=first_recv.at[kind, d],
            device_id=(sec, peer(d)),
            device_id_type=MESH,
        )

    def arrived(dst, sem):
        pltpu.make_async_remote_copy(
            src_ref=dst,
            dst_ref=dst,
            send_sem=first_send.at[0, 0],
            recv_sem=sem,
            device_id=(sec, peer(1)),
            device_id_type=MESH,
        ).wait_recv()

    def first_arrived(kind, d):
        source = flipped(d)
        spot = pl.ds(pl.multiple_of(source * toks, toks), toks)
        dst = (lambda: q_home.at[:, spot, :], lambda: h_in.at[spot])[kind]()
        arrived(dst, first_recv.at[kind, d])

    def new_copy(d, off, count):
        to = flipped(d)
        first, _ = duty_of(lax.rem(parity + off, 2), lax.rem(to, 2))
        spot = pl.ds(pl.multiple_of(off * block + a * toks, toks), toks)
        return pltpu.make_async_remote_copy(
            src_ref=kv_out.at[to, pl.ds(first, count)],
            dst_ref=kv_new.at[pl.ds(0, count), :, spot, :],
            send_sem=new_send.at[d, off],
            recv_sem=new_recv.at[0],
            device_id=(sec, along(-off, d)),
            device_id_type=MESH,
        )

    def each_new(act):
        for d in range(groups):
            for off in range(2):
                if d or off:
                    for count in (1, 2):

                        @pl.when(duty_of(lax.rem(parity + off, 2), lax.rem(a + d, 2))[1] == count)
                        def _(d=d, off=off, count=count):
                            act(new_copy(d, off, count))

    for d in range(1, groups):
        first_copy(0, d).start()

    def stale_copies(i):
        there, _ = duty_of(1 - parity, core)
        j = i - there
        head, tail = pl.ds(0, last), pl.ds(last, rows)
        head_at, tail_at = pl.ds(before_at, last), pl.ds(after_at, rows)
        deep = pl.ds(0, dim)
        return [
            pltpu.make_async_remote_copy(
                src_ref=src,
                dst_ref=dst,
                send_sem=kv_send.at[i, n],
                recv_sem=kv_recv.at[j, n],
                device_id=(sec, along(places)),
                device_id_type=MESH,
            )
            for n, (src, dst, places) in enumerate(
                (
                    (k_mine.at[i, head, :], k_site.at[j, head_at, :], 1),
                    (v_mine.at[i, :, head], v_site.at[j, deep, head_at], 1),
                    (k_mine.at[i, tail, :], k_site.at[j, tail_at, :], -1),
                    (v_mine.at[i, :, tail], v_site.at[j, deep, tail_at], -1),
                )
            )
        ]

    for i in range(heads):

        @pl.when(away(i) == 1)
        def _(i=i):
            for copy in stale_copies(i):
                copy.start()

    def own_part(j, carry):
        k_site[j, 0:stale_keys, :] = k_mine[first_head + j]
        v_site[j, 0:dim, 0:stale_keys] = v_mine[first_head + j]
        v_site[j, dim:, :] = jnp.ones_like(v_site[j, dim:, :])
        kv_new[j, :, mine, :] = kv_out[a, first_head + j]
        return carry

    lax.fori_loop(0, duty_count, own_part, 0)
    each_new(lambda copy: copy.start())

    def q_copy(i, off, k, piece):
        places = PLACES[off][k]
        there, _ = duty_of(lax.rem(parity + off, 2), core)
        j, slot = i - there, slot_of(SITES if places == SITES else -places)
        return pltpu.make_async_remote_copy(
            src_ref=q_home.at[i, pieces[piece], :],
            dst_ref=q_site.at[j, slot, pieces[piece], :],
            send_sem=q_send.at[i, k, piece],
            recv_sem=q_recv.at[j, slot, piece],
            device_id=(sec, along(places)),
            device_id_type=MESH,
        )

    def each_q(piece, act):
        for k in (3, 2, 1, 0):
            for i in range(heads):
                for off in range(2):
                    if PLACES[off][k]:

                        @pl.when(away(i) == off)
                        def _(i=i, off=off, k=k):
                            act(q_copy(i, off, k, piece))

    for piece, low, high in ((0, 1, 2), (1, 2, 4), (2, 4, groups)):
        for d in range(low, high):
            first_arrived(0, d)
        each_q(piece, lambda copy: copy.start())

    for d in range(1, groups):
        first_copy(1, d).start()

    def own_block(j, carry):
        q_site[j, 0] = q_home[first_head + j]
        return carry

    lax.fori_loop(0, duty_count, own_block, 0)

    got_gate.wait()
    picked = lax.broadcasted_iota(jnp.int32, gate_cols.shape, 0) == step[0]
    gate_row[...] = jnp.sum(
        jnp.where(picked, gate_cols[...].astype(F32), 0.0), axis=0, keepdims=True
    )

    def attend(p, j):
        q = q_site[j, 2 * p : 2 * p + 2].reshape(2 * block, dim)
        scores = lax.dot_general(
            k_site[j], q, (((1,), (1,)), ((), ())), preferred_element_type=F32
        )
        weights = jnp.exp(scores * (dim ** (-0.5))).astype(BF16)
        return jnp.dot(v_site[j], weights, preferred_element_type=F32)

    def back_copy(j, r):
        k = PLACES[r % 2].index(r if r == SITES else -r)
        return pltpu.make_async_remote_copy(
            src_ref=send.at[j, slot_of(r)],
            dst_ref=back.at[first_head + j, k],
            send_sem=back_send.at[j, slot_of(r)],
            recv_sem=back_recv.at[first_head + j, k],
            device_id=(sec, along(r)),
            device_id_type=MESH,
        )

    pairs = ((0, SITES), (1, -1), (2, -2), (3, -3))

    def keys_here(j, carry):
        head_at, tail_at = pl.ds(before_at, last), pl.ds(after_at, rows)
        arrived(k_site.at[j, head_at, :], kv_recv.at[j, 0])
        arrived(v_site.at[j, pl.ds(0, dim), head_at], kv_recv.at[j, 1])
        arrived(k_site.at[j, tail_at, :], kv_recv.at[j, 2])
        arrived(v_site.at[j, pl.ds(0, dim), tail_at], kv_recv.at[j, 3])
        return carry

    lax.fori_loop(0, duty_count, keys_here, 0)
    for count in (1, 2):

        @pl.when(duty_count == count)
        def _(count=count):
            arrived(kv_new.at[0:count, :, 0 : 2 * block - toks, :], new_recv.at[0])

    def fresh_here(j, carry):
        k_site[j, fresh_at:, :] = kv_new[j, 0]
        for n in range(2):
            spot = slice(n * block, (n + 1) * block)
            at = slice(fresh_at + n * block, fresh_at + (n + 1) * block)
            v_site[j, 0:dim, at] = kv_new[j, 1, spot, :].T
        return carry

    lax.fori_loop(0, duty_count, fresh_here, 0)

    for p in (0, 3, 2, 1):

        def work(j, carry, p=p):
            for r in pairs[p]:
                if r:
                    slot = slot_of(r)
                    for piece, spot in enumerate(pieces):
                        arrived(q_site.at[j, slot, spot, :], q_recv.at[j, slot, piece])
            total = attend(p, j)
            for n, r in enumerate(pairs[p]):
                piece = total[:, n * block : (n + 1) * block].astype(BF16)
                if r == 0:
                    back[first_head + j, 0] = piece
                else:
                    send[j, slot_of(r)] = piece
                    back_copy(j, r).start()
            return carry

        lax.fori_loop(0, duty_count, work, 0)

    got_h.wait()
    for d in range(1, groups):
        first_arrived(1, d)

    def out_copy(i, d):
        to = flipped(d)
        spot = pl.ds(pl.multiple_of(to * toks, toks), toks)
        cols = pl.ds(pl.multiple_of(a * width + i * dim, dim), dim)
        return pltpu.make_async_remote_copy(
            src_ref=mixed.at[i, spot, :],
            dst_ref=out.at[0, :, cols],
            send_sem=out_send.at[i, d],
            recv_sem=out_recv.at[0],
            device_id=(next_sec, peer(d)),
            device_id_type=MESH,
        )

    for i in range(heads):
        pl.when(away(i) == 1)(lambda i=i: arrived(back.at[i, 0], back_recv.at[i, 0]))
        for k in range(1, SITES):
            arrived(back.at[i, k], back_recv.at[i, k])
        total = sum(back[i, k].astype(F32) for k in range(SITES))
        attention = (total[0:dim] / total[dim : dim + 1]).T
        attention = attention.astype(BF16).astype(F32)
        cols = slice(i * dim, (i + 1) * dim)
        mixed[i] = (h_in[:, cols].astype(F32) + gate_row[:, cols] * attention).astype(BF16)
        for d in range(groups):
            out_copy(i, d).start()

    for kind in range(2):
        for d in range(1, groups):
            first_copy(kind, d).wait_send()
    each_new(lambda copy: copy.wait_send())
    for i in range(heads):

        @pl.when(away(i) == 1)
        def _(i=i):
            for copy in stale_copies(i):
                copy.wait_send()

    for piece in range(3):
        each_q(piece, lambda copy: copy.wait_send())

    def backs_sent(j, carry):
        for pair in pairs:
            for r in pair:
                if r:
                    back_copy(j, r).wait_send()
        return carry

    lax.fori_loop(0, duty_count, backs_sent, 0)
    for i in range(heads):
        for d in range(groups):
            out_copy(i, d).wait_send()
    arrived(out, out_recv.at[0])


def shards(sections, fresh_qkv, stale_cache, norm_gains, hidden, gate_table, patch_index, step_index):
    seq_count = lax.axis_size("seq")
    groups = HEAD_GROUPS
    ring = seq_count // groups
    toks, full = hidden.shape[1:]
    width = full // groups
    heads = width // HEAD_DIM
    dim = HEAD_DIM
    block = toks * groups
    patches, rows = stale_cache.shape[2:4]
    stale_keys = (patches - 1) * rows
    tall = dim + 16
    fresh = fresh_qkv.transpose(0, 2, 1, 3)
    hbm = pl.BlockSpec(memory_space=pltpu.HBM)
    smem = pl.BlockSpec(memory_space=pltpu.SMEM)
    dma = pltpu.SemaphoreType.DMA
    return pl.pallas_call(
        functools.partial(kernel, sections, seq_count),
        out_shape=jax.ShapeDtypeStruct(hidden.shape, BF16),
        in_specs=[hbm] * 5 + [smem] * 2,
        out_specs=pl.BlockSpec(memory_space=pl.ANY),
        scratch_shapes=[
            pltpu.VMEM((3, toks, full), BF16),
            pltpu.VMEM((patches, rows, 2 * width), BF16),
            pltpu.VMEM((2, dim), F32),
            pltpu.VMEM((gate_table.shape[1], width), BF16),
            pltpu.VMEM((1, width), F32),
            pltpu.VMEM((groups, heads, toks, dim), BF16),
            pltpu.VMEM((groups, heads, 2, toks, dim), BF16),
            pltpu.VMEM((heads, block, dim), BF16),
            pltpu.VMEM((block, width), BF16),
            pltpu.VMEM((heads, stale_keys, dim), BF16),
            pltpu.VMEM((heads, dim, stale_keys), BF16),
            pltpu.VMEM((2, ring, block, dim), BF16),
            pltpu.VMEM((2, 2 * (stale_keys + block), dim), BF16),
            pltpu.VMEM((2, tall, 2 * (stale_keys + block)), BF16),
            pltpu.VMEM((2, 2, 2 * block, dim), BF16),
            pltpu.VMEM((2, ring, tall, block), BF16),
            pltpu.VMEM((heads, SITES, tall, block), BF16),
            pltpu.VMEM((heads, block, dim), BF16),
            dma((5,)),
            dma((2, groups)),
            dma((2, groups)),
            dma((groups, 2)),
            dma((1,)),
            dma((heads, 4)),
            dma((2, 4)),
            dma((heads, SITES, 3)),
            dma((2, ring, 3)),
            dma((2, ring)),
            dma((heads, SITES)),
            dma((heads, groups)),
            dma((1,)),
        ],
        compiler_params=pltpu.CompilerParams(
            collective_id=0, has_side_effects=True, vmem_limit_bytes=24 * 1024 * 1024
        ),
    )(
        *(
            pltpu.with_memory_space_constraint(array, pltpu.HBM)
            for array in (
                fresh,
                stale_cache,
                norm_gains,
                hidden,
                gate_table,
            )
        ),
        patch_index,
        step_index,
    )


def solution(mesh):
    return jax.shard_map(
        functools.partial(shards, mesh.shape["section"]),
        mesh=mesh,
        in_specs=(
            P("section", "seq", None, None),
            P("section", "seq", None, None, None),
            P("section", None, None),
            P("section", "seq", None),
            P("section", None, None),
            P("section"),
            P("section"),
        ),
        out_specs=P("section", "seq", None),
        check_vma=False,
    )
```

time: 50.7 us -> 50.2 us (level)
  Pallas kernels: 48.7 us -> 48.1 us
where the time goes in v3:
time: 50.2 us; the launch traced here: 50.1 us
  Pallas kernels  48.1 us (96%)
  between operations  1.3 us (3%)
  local copies, waits for them, and re-layouts  0.64 us (1%)
    pallas_call x1, Pallas kernels, shards(): pl.pallas_call(functools.partial(kernel, sections, seq_count), out_shape=...  48.1 us

profile of v3, /device:TPU:1, one launch (start us, length us, event | category | flops | bytes accessed | tf_op | source)
XLA Modules:
  0.0 50.1 jit_solution(7622956642486255060)
XLA Ops:
  1.3 48.1 %shard_map.73 = bf16[1,16,3072]{2,1,0:T(8,128)(2,1)S(1)} custom-call(bf16[1,3,16,3072]{3,2,1,0:T(8,128)(2,1)} %bitcast.1, bf16[1,1,4,128,768]{4,3,2,1,0:T(8,128)(2,1)} %stale.1, f32[1,2,128]{2,1,0:T(2,128)} %gains_in.1, bf16[1,16,3072]{2,1,0:T(8,128)(2,1)} %hidden.1, bf16[1,50,3072]{2,1,0:T(8,128)(2,1)} %gate.1, s32[1]{0:T(128)S(6)} %copy.9.patch, ...), custom_call_target="tpu_custom_call" | custom-call | tf_op jit(solution)/shard_map/pallas_call | solution.py:469
  49.5 0.6 %copy.11 = bf16[1,16,3072]{2,1,0:T(8,128)(2,1)} copy(bf16[1,16,3072]{2,1,0:T(8,128)(2,1)S(1)} %shard_map.73) | data formatting | bytes 196608

commit v4 on v3

--- a/solution.py
+++ b/solution.py
@@ -53,7 +53,9 @@
     k_site,
     v_site,
     kv_new,
+    part,
     send,
+    mid,
     back,
     mixed,
     local_sem,
@@ -67,6 +69,8 @@
     q_recv,
     back_send,
     back_recv,
+    mid_send,
+    mid_recv,
     out_send,
     out_recv,
 ):
@@ -79,6 +83,7 @@
     block = groups * toks
     rows = old.shape[1]
     kept = old.shape[0] - 1
+    tall = send.shape[2]
     stale_keys = kept * rows
     last = (kept - 1) * rows
     before_at, after_at, fresh_at = stale_keys, stale_keys + last, 2 * stale_keys
@@ -273,6 +278,7 @@
         def _(i=i):
             for copy in stale_copies(i):
                 copy.start()
+            back[i, 2] = jnp.zeros_like(back[i, 2])
 
     def own_part(j, carry):
         k_site[j, 0:stale_keys, :] = k_mine[first_head + j]
@@ -297,8 +303,8 @@
             device_id_type=MESH,
         )
 
-    def each_q(piece, act):
-        for k in (3, 2, 1, 0):
+    def each_q(piece, act, order=(3, 2, 1, 0)):
+        for k in order:
             for i in range(heads):
                 for off in range(2):
                     if PLACES[off][k]:
@@ -310,8 +316,9 @@
     for piece, low, high in ((0, 1, 2), (1, 2, 4), (2, 4, groups)):
         for d in range(low, high):
             first_arrived(0, d)
-        each_q(piece, lambda copy: copy.start())
-
+        each_q(piece, lambda copy: copy.start(), (3, 2) if piece else (3, 2, 1, 0))
+    for piece in (1, 2):
+        each_q(piece, lambda copy: copy.start(), (1, 0))
     for d in range(1, groups):
         first_copy(1, d).start()
 
@@ -335,14 +342,35 @@
         weights = jnp.exp(scores * (dim ** (-0.5))).astype(BF16)
         return jnp.dot(v_site[j], weights, preferred_element_type=F32)
 
+    near = (2, -2, 1, -1)
+    cut = dim // 2
+
     def back_copy(j, r):
-        k = PLACES[r % 2].index(r if r == SITES else -r)
+        k = PLACES[r % 2].index(-r)
         return pltpu.make_async_remote_copy(
             src_ref=send.at[j, slot_of(r)],
             dst_ref=back.at[first_head + j, k],
             send_sem=back_send.at[j, slot_of(r)],
             recv_sem=back_recv.at[first_head + j, k],
             device_id=(sec, along(r)),
+            device_id_type=MESH,
+        )
+
+    hops = (
+        (SITES, 2, 2, pl.ds(0, cut)),
+        (SITES, -2, -2, pl.ds(cut, tall - cut)),
+        (3, 2, 1, pl.ds(0, tall)),
+        (-3, -2, -1, pl.ds(0, tall)),
+    )
+
+    def mid_copy(j, hop):
+        r, way, there, spot = hops[hop]
+        return pltpu.make_async_remote_copy(
+            src_ref=send.at[j, slot_of(r), spot, :],
+            dst_ref=mid.at[j, hop, spot, :],
+            send_sem=mid_send.at[j, hop],
+            recv_sem=mid_recv.at[j, hop],
+            device_id=(sec, along(way)),
             device_id_type=MESH,
         )
 
@@ -383,15 +411,35 @@
                         arrived(q_site.at[j, slot, spot, :], q_recv.at[j, slot, piece])
             total = attend(p, j)
             for n, r in enumerate(pairs[p]):
-                piece = total[:, n * block : (n + 1) * block].astype(BF16)
+                sums = total[:, n * block : (n + 1) * block]
                 if r == 0:
-                    back[first_head + j, 0] = piece
+                    back[first_head + j, 0] = sums.astype(BF16)
+                elif r in near:
+                    part[j, near.index(r)] = sums
                 else:
-                    send[j, slot_of(r)] = piece
-                    back_copy(j, r).start()
+                    send[j, slot_of(r)] = sums.astype(BF16)
+                    for hop in range(len(hops)):
+                        if hops[hop][0] == r:
+                            mid_copy(j, hop).start()
             return carry
 
         lax.fori_loop(0, duty_count, work, 0)
+
+    for hop, (_, _, r, spot) in enumerate(hops):
+
+        def add_on(j, carry, hop=hop, r=r, spot=spot):
+            arrived(mid.at[j, hop, spot, :], mid_recv.at[j, hop])
+            n = near.index(r)
+            sums = part[j, n, spot, :] + mid[j, hop, spot, :].astype(F32)
+            send[j, slot_of(r), spot, :] = sums.astype(BF16)
+            if r == 2:
+                send[j, slot_of(r), cut:, :] = part[j, n, cut:, :].astype(BF16)
+            if r == -2:
+                send[j, slot_of(r), 0:cut, :] = part[j, n, 0:cut, :].astype(BF16)
+            back_copy(j, r).start()
+            return carry
+
+        lax.fori_loop(0, duty_count, add_on, 0)
 
     got_h.wait()
     for d in range(1, groups):
@@ -412,9 +460,9 @@
 
     for i in range(heads):
         pl.when(away(i) == 1)(lambda i=i: arrived(back.at[i, 0], back_recv.at[i, 0]))
-        for k in range(1, SITES):
-            arrived(back.at[i, k], back_recv.at[i, k])
-        total = sum(back[i, k].astype(F32) for k in range(SITES))
+        arrived(back.at[i, 1], back_recv.at[i, 1])
+        pl.when(away(i) == 0)(lambda i=i: arrived(back.at[i, 2], back_recv.at[i, 2]))
+        total = sum(back[i, k].astype(F32) for k in range(3))
         attention = (total[0:dim] / total[dim : dim + 1]).T
         attention = attention.astype(BF16).astype(F32)
         cols = slice(i * dim, (i + 1) * dim)
@@ -437,10 +485,9 @@
         each_q(piece, lambda copy: copy.wait_send())
 
     def backs_sent(j, carry):
-        for pair in pairs:
-            for r in pair:
-                if r:
-                    back_copy(j, r).wait_send()
+        for n in range(4):
+            back_copy(j, near[n]).wait_send()
+            mid_copy(j, n).wait_send()
         return carry
 
     lax.fori_loop(0, duty_count, backs_sent, 0)
@@ -487,8 +534,10 @@
             pltpu.VMEM((2, 2 * (stale_keys + block), dim), BF16),
             pltpu.VMEM((2, tall, 2 * (stale_keys + block)), BF16),
             pltpu.VMEM((2, 2, 2 * block, dim), BF16),
+            pltpu.VMEM((2, 4, tall, block), F32),
             pltpu.VMEM((2, ring, tall, block), BF16),
-            pltpu.VMEM((heads, SITES, tall, block), BF16),
+            pltpu.VMEM((2, 4, tall, block), BF16),
+            pltpu.VMEM((heads, 3, tall, block), BF16),
             pltpu.VMEM((heads, block, dim), BF16),
             dma((5,)),
             dma((2, groups)),
@@ -500,7 +549,9 @@
             dma((heads, SITES, 3)),
             dma((2, ring, 3)),
             dma((2, ring)),
-            dma((heads, SITES)),
+            dma((heads, 3)),
+            dma((2, 4)),
+            dma((2, 4)),
             dma((heads, groups)),
             dma((1,)),
         ],

time: 50.2 us -> 49.8 us (level)
  no operation moved by 1% of the time
where the time goes in v4:
time: 49.8 us; the launch traced here: 49.7 us
  Pallas kernels  47.7 us (96%)
  between operations  1.3 us (3%)
  local copies, waits for them, and re-layouts  0.64 us (1%)
    pallas_call x1, Pallas kernels, shards(): pl.pallas_call(functools.partial(kernel, sections, seq_count), out_shape=...  47.7 us

profile of v4, /device:TPU:1, one launch (start us, length us, event | category | flops | bytes accessed | tf_op | source)
XLA Modules:
  0.0 49.7 jit_solution(1185596653981564255)
XLA Ops:
  1.3 47.7 %shard_map.73 = bf16[1,16,3072]{2,1,0:T(8,128)(2,1)S(1)} custom-call(bf16[1,3,16,3072]{3,2,1,0:T(8,128)(2,1)} %bitcast.1, bf16[1,1,4,128,768]{4,3,2,1,0:T(8,128)(2,1)} %stale.1, f32[1,2,128]{2,1,0:T(2,128)} %gains_in.1, bf16[1,16,3072]{2,1,0:T(8,128)(2,1)} %hidden.1, bf16[1,50,3072]{2,1,0:T(8,128)(2,1)} %gate.1, s32[1]{0:T(128)S(6)} %copy.9.patch, ...), custom_call_target="tpu_custom_call" | custom-call | tf_op jit(solution)/shard_map/pallas_call | solution.py:516
  49.0 0.6 %copy.11 = bf16[1,16,3072]{2,1,0:T(8,128)(2,1)} copy(bf16[1,16,3072]{2,1,0:T(8,128)(2,1)S(1)} %shard_map.73) | data formatting | bytes 196608

commit v5 on v4

--- a/solution.py
+++ b/solution.py
@@ -128,16 +128,20 @@
         )
     ]
 
+    far_first = sorted(range(groups), key=lambda d: -(d // 2 == 2) * 2 - (d > 1))
+
     barrier = pltpu.get_barrier_semaphore()
 
     def greet(section, seq):
         pl.semaphore_signal(barrier, inc=1, device_id=(section, seq), device_id_type=MESH)
 
-    for d in range(groups - 1, 0, -1):
-        greet(sec, along(0, d))
-    for d in range(groups - 1, -1, -1):
+    for d in far_first:
         greet(sec, along(1, d))
-    for r in (4, 3, -3, 2, -2, -1):
+        if d:
+            greet(sec, along(0, d))
+        if d == far_first[1]:
+            greet(sec, along(4))
+    for r in (3, -3, 2, -2, -1):
         greet(sec, along(r))
     greet(prev_sec, me)
     greeted = 2 * groups + 6
@@ -467,7 +471,7 @@
         attention = attention.astype(BF16).astype(F32)
         cols = slice(i * dim, (i + 1) * dim)
         mixed[i] = (h_in[:, cols].astype(F32) + gate_row[:, cols] * attention).astype(BF16)
-        for d in range(groups):
+        for d in far_first:
             out_copy(i, d).start()
 
     for kind in range(2):

time: 49.8 us -> 50 us (level)
  no operation moved by 1% of the time
where the time goes in v5:
time: 50 us; the launch traced here: 49.9 us
  Pallas kernels  47.9 us (96%)
  between operations  1.3 us (3%)
  local copies, waits for them, and re-layouts  0.64 us (1%)
    pallas_call x1, Pallas kernels, shards(): pl.pallas_call(functools.partial(kernel, sections, seq_count), out_shape=...  47.9 us

profile of v5, /device:TPU:1, one launch (start us, length us, event | category | flops | bytes accessed | tf_op | source)
XLA Modules:
  0.0 49.9 jit_solution(6567776151453838290)
XLA Ops:
  1.3 47.9 %shard_map.73 = bf16[1,16,3072]{2,1,0:T(8,128)(2,1)S(1)} custom-call(bf16[1,3,16,3072]{3,2,1,0:T(8,128)(2,1)} %bitcast.1, bf16[1,1,4,128,768]{4,3,2,1,0:T(8,128)(2,1)} %stale.1, f32[1,2,128]{2,1,0:T(2,128)} %gains_in.1, bf16[1,16,3072]{2,1,0:T(8,128)(2,1)} %hidden.1, bf16[1,50,3072]{2,1,0:T(8,128)(2,1)} %gate.1, s32[1]{0:T(128)S(6)} %copy.9.patch, ...), custom_call_target="tpu_custom_call" | custom-call | tf_op jit(solution)/shard_map/pallas_call | solution.py:520
  49.2 0.6 %copy.11 = bf16[1,16,3072]{2,1,0:T(8,128)(2,1)} copy(bf16[1,16,3072]{2,1,0:T(8,128)(2,1)S(1)} %shard_map.73) | data formatting | bytes 196608
